TPU v7x, 32 devices: a whole 2x2x4 slice. The times are simulated.
32 devices in a mesh: grp: 2 (over core), seq: 4 (over y, x), tp: 4 (over z).
Axes of the slice: x: 2, y: 2, z: 4, core: 2. Of those that a mesh axis runs over, the one named last changes fastest.
Arguments:
- prompt: bfloat16 [4096, 8192], P(('grp', 'seq'), 'tp'), may hold values from -6 to 6
- w_kv: bfloat16 [8192, 2048], P(None, 'tp'), may hold values from -0.0625 to 0.0625
- block_owner: int32 [512, 1], P(('grp', 'seq')), may hold values from 0 to 7, as said below
- block_row: int32 [512], P(('grp', 'seq')), may hold values from 0 to 31, as said below
- queries: bfloat16 [256, 4, 8192], P(('grp', 'seq'), None, 'tp'), may hold values from -150 to 150
- new_kv: bfloat16 [256, 4, 2048], P(('grp', 'seq'), None, 'tp'), may hold values from -6 to 6
- cache_codes: bfloat16 [256, 128, 2048], P(('grp', 'seq'), None, 'tp'), may hold values from -4 to 4
- cache_scales: float32 [256, 8, 16], P(('grp', 'seq'), None, 'tp'), may hold values from 0.5 to 2
- lengths: int32 [256], P(('grp', 'seq')), may hold values from 1 to 128, 16384 in all
- w_out: bfloat16 [8192, 8192], P('tp', 'seq'), may hold values from -0.5 to 0.5
Outputs:
- mixed: bfloat16 [1024, 8192], P(('grp', 'tp'), 'seq')
Inputs may be any that keep to these rules, and one draw needn't show every extreme that they name: `block_owner`: the blocks come in aligned groups of 8 consecutive blocks that share one owner and one request; the groups of one prefill device all go to different owners, so a prefill device sends exactly 8 blocks to each owner it sends to. `block_row`: equal on all blocks of one aligned group of 8 blocks.
All inputs are finite; a program needn't handle non-finite values. No bound on the sum of `lengths` on one device may be relied on, other than what follows from the above.
Results may differ from a plain program's by a relative error of at most 0.014.
Values may be sent and summed in bfloat16 or wider, within the bound.
A program may use at most 256 MiB of HBM per device.

v0:
```python
import math

import jax
import jax.numpy as jnp
from jax import lax
from jax.sharding import PartitionSpec as P

HQ = 64
KVH = 8
HD = 128
NEW = 4
BLK = 8
CBLK = 16
CAP = 8


EPS = 1e-05


def on_device(
    prompt, w_kv, block_owner, block_row, queries, new_kv, cache_codes, cache_scales, lengths, w_out
):
    group_count = lax.axis_size("grp")
    seq_count = lax.axis_size("seq")
    owners = group_count * seq_count
    tokens = prompt.shape[0]
    features = w_kv.shape[0]
    columns = w_kv.shape[1]
    row_count = queries.shape[0]
    shard_piece = lax.all_gather(prompt, "tp", axis=1, tiled=True)
    running = jnp.dot(shard_piece, w_kv, preferred_element_type=jnp.float32)
    widened = shard_piece.astype(jnp.float32)
    squares = jnp.sum(widened * widened, axis=1)
    row_scale = lax.rsqrt(squares / features + EPS)
    prompt_kv = (running * row_scale[:, None]).astype(jnp.bfloat16)
    blocks = tokens // BLK
    capacity = CAP
    owner_ids = block_owner[:, 0]
    owner_onehot = (owner_ids[:, None] == jnp.arange(owners, dtype=jnp.int32)[None, :]).astype(
        jnp.int32
    )
    slot_rank = jnp.sum((jnp.cumsum(owner_onehot, axis=0) - owner_onehot) * owner_onehot, axis=1)
    target = owner_ids * capacity + slot_rank
    chosen = target[None, :] == jnp.arange(owners * capacity, dtype=jnp.int32)[:, None]
    packed = jnp.dot(
        chosen.astype(jnp.bfloat16),
        prompt_kv.reshape(blocks, BLK * columns),
        preferred_element_type=jnp.float32,
    )
    send_kv = packed.astype(jnp.bfloat16).reshape(owners, capacity, BLK, columns)
    send_rows = (jnp.sum(jnp.where(chosen, block_row[None, :] + 1, 0), axis=1) - 1).reshape(
        owners, capacity
    )
    arrived_kv, arrived_rows = (
        lax.all_to_all(send_kv, ("grp", "seq"), split_axis=0, concat_axis=0, tiled=True),
        lax.all_to_all(send_rows, ("grp", "seq"), split_axis=0, concat_axis=0, tiled=True),
    )
    slots = arrived_rows.shape[1]
    kv_heads = columns // (2 * HD)
    head_group = HQ // KVH
    context = cache_codes.shape[1]
    query_heads = queries.reshape(row_count, NEW, kv_heads, head_group, HD)
    fresh_kv = new_kv.reshape(row_count, NEW, kv_heads, 2, HD)
    stored = cache_codes.reshape(row_count, context, kv_heads, 2, HD)
    block_scales = cache_scales.reshape(row_count, context // CBLK, kv_heads, 2)
    key_scale = jnp.transpose(jnp.repeat(block_scales[:, :, :, 0], CBLK, axis=1), (0, 2, 1))
    value_scale = jnp.transpose(jnp.repeat(block_scales[:, :, :, 1], CBLK, axis=1), (0, 2, 1))
    arrived = arrived_kv.reshape(owners * slots * BLK, kv_heads, 2, HD)
    arrived_targets = jnp.broadcast_to(arrived_rows[:, :, None], (owners, slots, BLK)).reshape(
        owners * slots * BLK
    )
    inverse_root = 1.0 / math.sqrt(HD)
    row_ids = jnp.arange(row_count, dtype=jnp.int32)
    s_cache = jnp.einsum(
        "rinhd,rpnd->rinhp", query_heads, stored[:, :, :, 0, :], preferred_element_type=jnp.float32
    )
    s_cache = s_cache * key_scale[:, None, :, None, :] * inverse_root
    cache_live = jnp.arange(context, dtype=jnp.int32)[None, :] < lengths[:, None]
    s_cache = jnp.where(cache_live[:, None, None, None, :], s_cache, -jnp.inf)
    s_sent = (
        jnp.einsum(
            "rinhd,knd->rinhk", query_heads, arrived[:, :, 0, :], preferred_element_type=jnp.float32
        )
        * inverse_root
    )
    sent_live = arrived_targets[None, :] == row_ids[:, None]
    s_sent = jnp.where(sent_live[:, None, None, None, :], s_sent, -jnp.inf)
    s_fresh = (
        jnp.einsum(
            "rinhd,rjnd->rinhj",
            query_heads,
            fresh_kv[:, :, :, 0, :],
            preferred_element_type=jnp.float32,
        )
        * inverse_root
    )
    causal = jnp.arange(NEW)[None, :] <= jnp.arange(NEW)[:, None]
    s_fresh = jnp.where(causal[None, :, None, None, :], s_fresh, -jnp.inf)
    row_max = jnp.maximum(
        jnp.maximum(jnp.max(s_cache, axis=-1), jnp.max(s_sent, axis=-1)), jnp.max(s_fresh, axis=-1)
    )
    w_cache = jnp.exp(s_cache - row_max[..., None])
    w_sent = jnp.exp(s_sent - row_max[..., None])
    w_fresh = jnp.exp(s_fresh - row_max[..., None])
    denominator = jnp.sum(w_cache, axis=-1) + jnp.sum(w_sent, axis=-1) + jnp.sum(w_fresh, axis=-1)
    cache_weights = (w_cache * value_scale[:, None, :, None, :]).astype(jnp.bfloat16)
    numerator = jnp.einsum(
        "rinhp,rpnd->rinhd",
        cache_weights,
        stored[:, :, :, 1, :],
        preferred_element_type=jnp.float32,
    )
    numerator = numerator + jnp.einsum(
        "rinhk,knd->rinhd",
        w_sent.astype(jnp.bfloat16),
        arrived[:, :, 1, :],
        preferred_element_type=jnp.float32,
    )
    numerator = numerator + jnp.einsum(
        "rinhj,rjnd->rinhd",
        w_fresh.astype(jnp.bfloat16),
        fresh_kv[:, :, :, 1, :],
        preferred_element_type=jnp.float32,
    )
    attention = (
        (numerator / denominator[..., None])
        .astype(jnp.bfloat16)
        .reshape(row_count * NEW, kv_heads * head_group * HD)
    )
    head_terms = jnp.dot(
        lax.all_gather(attention, "seq", axis=0, tiled=True),
        w_out,
        preferred_element_type=jnp.float32,
    )
    return lax.psum_scatter(head_terms.astype(jnp.bfloat16), "tp", scatter_dimension=0, tiled=True)


def solution(mesh):
    in_specs = (
        P(("grp", "seq"), "tp"),
        P(None, "tp"),
        P(("grp", "seq"), None),
        P(("grp", "seq")),
        P(("grp", "seq"), None, "tp"),
        P(("grp", "seq"), None, "tp"),
        P(("grp", "seq"), None, "tp"),
        P(("grp", "seq"), None, "tp"),
        P(("grp", "seq")),
        P("tp", "seq"),
    )
    out_specs = P(("grp", "tp"), "seq")
    return jax.shard_map(
        on_device, mesh=mesh, in_specs=in_specs, out_specs=out_specs, check_vma=False
    )
```

profile of v0, /device:TPU:6, one launch (start us, length us, event | category | flops | bytes accessed | tf_op | source)
XLA Modules:
  0.0 295.2 jit_solution(8916074630826948876)
XLA Ops:
  6.5 0.0 all-gather.3.cloned.1.call-start
  6.5 0.7 all-gather.3.cloned.1.call-update
  7.3 0.7 fusion.33
  8.0 0.1 reduce_window_sum.11
  8.1 0.8 select_reduce_fusion.1
  8.9 0.7 broadcast_add_fusion.1
  9.6 0.7 multiply_add_fusion
  10.2 0.1 select_reduce_fusion
  10.4 0.7 sub.35
  11.1 4.2 %all-to-all-start = ((s32[8,1,8]{2,1,0:T(1,128)}), s32[8,1,8]{2,1,0:T(1,128)S(1)}, u32[]{:S(2)}, u32[]{:S(2)}) async-start(s32[8,1,8]{2,1,0:T(1,128)} %bitcast.10), calls=%async_computation | async-start | bytes 8192 | tf_op jit(solution)/shard_map/all_to_all | solution.py:56
  15.3 1.4 reshape.131
  16.6 0.0 copy-start.4
  16.6 0.0 copy-start.2
  16.7 0.0 copy-start.5
  16.7 6.8 %copy.81 = bf16[32,128,512]{1,2,0:T(8,128)(2,1)} copy(bf16[32,128,512]{2,1,0:T(8,128)(2,1)} %param.16) | data formatting | bytes 8388608 | tf_op args[6]
  23.4 0.0 copy-done.4
  23.5 0.1 copy.85
  23.6 0.0 copy-done.2
  23.6 0.1 reshape.146
  23.7 0.1 copy.95
  23.7 0.0 copy-done.5
  23.8 0.1 iota_compare_fusion.4
  23.8 0.8 fusion.36
  24.7 2.4 fusion.39
  27.1 132.7 %all-gather.3.cloned.1.call-done = bf16[512,8192]{1,0:T(8,128)(2,1)} async-done(((bf16[512,2048]{1,0:T(8,128)(2,1)}), bf16[512,8192]{1,0:T(8,128)(2,1)}) %all-gather.3.cloned.1.call-update) | async-done | bytes 8388624 | tf_op jit(solution)/shard_map/all_gather | solution.py:30
  159.8 0.0 copy-start.1
  159.8 5.3 %multiply_reduce_fusion = f32[512]{0:T(512)S(1)} fusion(bf16[512,8192]{1,0:T(8,128)(2,1)} %all-gather.3.cloned.1.call-done), kind=kLoop, calls=%fused_computation | loop fusion | flops 12582400 | bytes 8390656 | tf_op jit(solution)/shard_map/reduce_sum | solution.py:33
  165.0 0.5 copy-done.1
  165.6 7.1 %fusion.19 = bf16[512,512]{1,0:T(8,128)(2,1)S(1)} fusion(bf16[512,8192]{1,0:T(8,128)(2,1)S(1)} %copy-done.1, bf16[8192,512]{1,0:T(8,128)(2,1)} %param.11, f32[512]{0:T(512)S(1)} %add_rsqrt_fusion), kind=kOutput, calls=%fused_computation.26 | convolution fusion | flops 4295491584 | bytes 17303552 | tf_op jit(solution)/shard_map/dot_general | solution.py:31
  172.6 0.2 reshape.134
  172.9 0.3 convolution_convert_fusion
  173.2 1.0 copy.87
  174.2 0.0 all-to-all-done
  174.2 4.2 %all-to-all-start.1 = ((bf16[8,8,8,512]{3,2,1,0:T(8,128)(2,1)}), bf16[8,8,8,512]{3,2,1,0:T(8,128)(2,1)S(1)}, u32[]{:S(2)}, u32[]{:S(2)}) async-start(bf16[8,8,8,512]{3,2,1,0:T(8,128)(2,1)} %copy.87), calls=%async_computation.1 | async-start | bytes 1048576 | tf_op jit(solution)/shard_map/all_to_all | solution.py:55
  178.4 0.0 all-gather.5.cloned.1.call-start
  178.4 4.0 %fusion.38 = (f32[32,4,2,8]{3,1,2,0:T(4,128)}, f32[32,4,2,8,4]{3,4,1,2,0:T(4,128)S(1)}) fusion(bf16[32,4,2,8,128]{4,3,2,1,0:T(8,128)(2,1)S(1)} %reshape.131, bf16[32,4,2,1,128]{4,3,2,1,0:T(2,128)(2,1)} %get-tuple-element.10, pred[4,4]{1,0:T(4,128)(4,1)S(1)} %iota_compare_fusion.5), kind=kOutput, calls=%fused_computation.65 | convolution fusion | flops 2119680 | bytes 630800 | tf_op jit(solution)/shard_map/rinhd,rjnd->rinhj/dot_general | solution.py:89
  182.4 0.1 broadcast_in_dim.87
  182.4 0.1 eq.51
  182.6 3.2 %all-to-all-done.1 = bf16[8,8,8,512]{3,2,1,0:T(8,128)(2,1)S(1)} async-done(((bf16[8,8,8,512]{3,2,1,0:T(8,128)(2,1)}), bf16[8,8,8,512]{3,2,1,0:T(8,128)(2,1)S(1)}, u32[]{:S(2)}, u32[]{:S(2)}) %all-to-all-start.1) | async-done | bytes 524320 | tf_op jit(solution)/shard_map/all_to_all | solution.py:55
  185.8 0.1 reshape.136
  185.9 0.7 fusion.35
  186.6 0.0 copy-start.3
  186.7 2.9 fusion.2
  189.6 0.1 copy.90
  189.7 0.0 copy-done.3
  189.7 0.1 copy.98
  189.8 3.7 %fusion = (f32[32,4,2,8]{0,3,1,2:T(8,128)S(1)}, bf16[32,4,2,8,512]{4,0,3,1,2:T(8,128)(2,1)}) fusion(f32[2,512,32,4,8]{1,2,4,3,0:T(8,128)} %get-tuple-element.18, f32[32,4,2,8]{0,3,1,2:T(8,128)S(1)} %copy.98, pred[32,512]{1,0:T(8,128)(4,1)S(1)} %iota_compare_fusion), kind=kLoop, calls=%fused_computation.4 | loop fusion | flops 5240832 | bytes 6324224 | tf_op jit(solution)/shard_map/reduce_sum | solution.py:105
  193.6 0.1 copy.101
  193.7 0.8 fusion.22
  194.5 0.5 fusion.29
  194.9 0.0 copy-start
  194.9 3.2 %fusion.8 = f32[32,4,2,8,128]{4,3,1,2,0:T(8,128)S(1)} fusion(bf16[32,4,2,8,512]{4,0,3,1,2:T(8,128)(2,1)} %get-tuple-element.6, bf16[512,2,1,128]{3,2,1,0:T(2,128)(2,1)S(1)} %get-tuple-element.7), kind=kOutput, calls=%fused_computation.16 | convolution fusion | flops 268435456 | bytes 3407872 | tf_op jit(solution)/shard_map/rinhk,knd->rinhd/dot_general | solution.py:113
  198.1 0.0 copy-done
  198.1 1.2 fusion.13
  199.4 0.6 fusion.18
  200.0 0.1 copy.102
  200.1 1.0 reshape.139
  201.1 0.0 all-gather.5.cloned.1.call-update
  201.2 0.0 reduce-scatter.2.cloned.1.call-start
  201.2 32.7 %all-gather.5.cloned.1.call-done = bf16[512,2048]{1,0:T(8,128)(2,1)} async-done(((bf16[128,2048]{1,0:T(8,128)(2,1)}), bf16[512,2048]{1,0:T(8,128)(2,1)}) %all-gather.5.cloned.1.call-update) | async-done | bytes 2097168 | tf_op jit(solution)/shard_map/all_gather | solution.py:131
  233.9 9.8 %convolution_convert_fusion.1 = bf16[512,2048]{1,0:T(8,128)(2,1)} fusion(bf16[512,2048]{1,0:T(8,128)(2,1)} %all-gather.5.cloned.1.call-done, bf16[2048,2048]{1,0:T(8,128)(2,1)} %param.19), kind=kOutput, calls=%fused_computation.7 | convolution fusion | flops 4296015872 | bytes 12582912 | tf_op jit(solution)/shard_map/dot_general | solution.py:130
  243.7 0.0 reduce-scatter.2.cloned.1.call-update
  243.7 44.9 %reduce-scatter.2.cloned.1.call-done = bf16[128,2048]{1,0:T(8,128)(2,1)} async-done(((bf16[512,2048]{1,0:T(8,128)(2,1)}), bf16[128,2048]{1,0:T(8,128)(2,1)}) %reduce-scatter.2.cloned.1.call-update) | async-done | bytes 524304 | tf_op jit(solution)/shard_map/reduce_scatter | solution.py:135
  (11 shorter events, 0.1 us)
Async XLA Ops:
  6.5 153.2 %all-gather.3.cloned.1.call-start = ((), (), s32[]{:S(2)}) async-start(), calls=%async_computation.3 | async-start | bytes 10485760 | tf_op jit(solution)/shard_map/all_gather | solution.py:30
  11.1 163.1 %all-to-all-start = ((s32[8,1,8]{2,1,0:T(1,128)}), s32[8,1,8]{2,1,0:T(1,128)S(1)}, u32[]{:S(2)}, u32[]{:S(2)}) async-start(s32[8,1,8]{2,1,0:T(1,128)} %bitcast.10), calls=%async_computation | async-start | bytes 8192 | tf_op jit(solution)/shard_map/all_to_all | solution.py:56
  16.6 6.8 %copy-start.4 = (f32[32,8,4]{0,2,1:T(4,128)S(1)}, f32[32,8,4]{0,2,1:T(4,128)}, u32[]{:S(2)}) copy-start(f32[32,8,4]{0,2,1:T(4,128)} %param.17) | copy-start | bytes 12292
  16.6 6.9 %copy-start.2 = (bf16[32,4,512]{2,1,0:T(4,128)(2,1)S(1)}, bf16[32,4,512]{2,1,0:T(4,128)(2,1)}, u32[]{:S(2)}) copy-start(bf16[32,4,512]{2,1,0:T(4,128)(2,1)} %param.15) | copy-start | bytes 393220
  16.7 7.1 %copy-start.5 = (s32[32]{0:T(128)S(1)}, s32[32]{0:T(128)}, u32[]{:S(2)}) copy-start(s32[32]{0:T(128)} %param.18) | copy-start | bytes 388
  159.8 5.8 %copy-start.1 = (bf16[512,8192]{1,0:T(8,128)(2,1)S(1)}, bf16[512,8192]{1,0:T(8,128)(2,1)}, u32[]{:S(2)}) copy-start(bf16[512,8192]{1,0:T(8,128)(2,1)} %all-gather.3.cloned.1.call-done) | copy-start | bytes 25165828
  174.2 11.6 %all-to-all-start.1 = ((bf16[8,8,8,512]{3,2,1,0:T(8,128)(2,1)}), bf16[8,8,8,512]{3,2,1,0:T(8,128)(2,1)S(1)}, u32[]{:S(2)}, u32[]{:S(2)}) async-start(bf16[8,8,8,512]{3,2,1,0:T(8,128)(2,1)} %copy.87), calls=%async_computation.1 | async-start | bytes 1048576 | tf_op jit(solution)/shard_map/all_to_all | solution.py:55
  178.4 55.6 %all-gather.5.cloned.1.call-start = ((), (), s32[]{:S(2)}) async-start(), calls=%async_computation.4 | async-start | bytes 2621440 | tf_op jit(solution)/shard_map/all_gather | solution.py:131
  186.6 3.1 %copy-start.3 = (f32[32,4,2,8]{3,1,2,0:T(4,128)S(1)}, f32[32,4,2,8]{3,1,2,0:T(4,128)}, u32[]{:S(2)}) copy-start(f32[32,4,2,8]{3,1,2,0:T(4,128)} %get-tuple-element.13) | copy-start | bytes 24580
  194.9 3.2 %copy-start = (bf16[32,128,512]{1,2,0:T(8,128)(2,1)S(1)}, bf16[32,128,512]{1,2,0:T(8,128)(2,1)}, u32[]{:S(2)}) copy-start(bf16[32,128,512]{1,2,0:T(8,128)(2,1)} %copy.81) | copy-start | bytes 12582916
  201.2 87.5 %reduce-scatter.2.cloned.1.call-start = ((), (), s32[]{:S(2)}) async-start(), calls=%async_computation.5 | async-start | bytes 2621440 | tf_op jit(solution)/shard_map/reduce_scatter | solution.py:135
Sparse Core Ops, SparseCore 0:
  8.9 150.8 all-gather.2
  201.3 32.5 all-gather.4
  243.9 44.7 reduce-scatter.1
where the time goes:
time: 297 us; the launch traced here: 295 us
  waiting for transfers between devices  214 us (72%)
  matrix products  31.5 us (11%)
  local copies, waits for them, and re-layouts  14.1 us (5%)
  other arithmetic  13.5 us (5%)
  between operations  13.4 us (5%)
  starting transfers between devices  8.44 us (3%)
    all_gather x1, waiting for transfers between devices, on_device(): shard_piece = lax.all_gather(prompt, 'tp', axis=1, tiled=True)  133 us
    reduce_scatter x1, waiting for transfers between devices, on_device(): lax.psum_scatter(head_terms.astype(jnp.bfloat16), 'tp', scatter_dimension...  44.9 us
    all_gather x1, waiting for transfers between devices, on_device(): lax.all_gather(attention, 'seq', axis=0, tiled=True)  32.7 us
    dot_general x1, matrix products, on_device(): jnp.dot(lax.all_gather(attention, 'seq', axis=0, tiled=True), w_out, pref...  9.81 us
    unnamed x13, local copies, waits for them, and re-layouts  7.3 us
    dot_general x1, matrix products, on_device(): running = jnp.dot(shard_piece, w_kv, preferred_element_type=jnp.float32)  7.08 us
  transfers between devices with their start and end apart: 5, of which 4 were waited for; matrix products, arithmetic and copies ran while one was open for 11% of the time, Pallas kernels for 0%

commit v1 on v0

v1 whole, which is shorter than its diff:
```python
import functools
import math

import jax
import jax.numpy as jnp
from jax import lax
from jax.experimental import pallas as pl
from jax.experimental.pallas import tpu as pltpu
from jax.sharding import PartitionSpec as P

HQ = 64
KVH = 8
HD = 128
NEW = 4
BLK = 8
CBLK = 16
CAP = 8
GT = BLK * CAP

EPS = 1e-05
MESH = pl.DeviceIdType.MESH
MIB = 1 << 20


def remote(src, dst, send_sem, recv_sem, **where):
    return pltpu.make_async_remote_copy(
        src_ref=src, dst_ref=dst, send_sem=send_sem, recv_sem=recv_sem, device_id=where, device_id_type=MESH
    )


def project_kernel(
    n_grp, n_seq, n_tp,
    match_ref, x_ref, w_ref, ss_ref, rows_ref, pick_ref,
    akv_ref, ameta_ref,
    wbuf, own, pbuf, rbuf, ssbuf, sstot, kvbuf, stage, mstage, kland, mland,
    local_sem, zs, zr, ps, pr, gs, gr, ds, dr, ss_s, ss_r, ks, kr, ms, mr,
):
    me_g, me_s, me_t = lax.axis_index("grp"), lax.axis_index("seq"), lax.axis_index("tp")
    owners = n_grp * n_seq
    me_o = me_g * n_seq + me_s
    features = x_ref.shape[1]
    part = features // owners
    groups = x_ref.shape[0] // GT
    waits = []

    def rows_of(g, s):
        return pl.ds(pl.multiple_of((g * n_seq + s) * part, part), part)

    local = pltpu.make_async_copy(
        w_ref.at[pl.ds(pl.multiple_of(me_t * features, features), features), :], wbuf.at[me_t], local_sem
    )
    local.start()

    barrier = pltpu.get_barrier_semaphore()
    for k in range(1, n_tp):
        pl.semaphore_signal(barrier, inc=1, device_id={"tp": lax.rem(me_t + k, n_tp)}, device_id_type=MESH)
    for j in range(1, owners):
        o = lax.rem(me_o + j, owners)
        pl.semaphore_signal(
            barrier, inc=1, device_id={"grp": o // n_seq, "seq": lax.rem(o, n_seq)}, device_id_type=MESH
        )
    pl.semaphore_wait(barrier, n_tp - 1 + owners - 1)

    for k in range(1, n_tp):
        t = lax.rem(me_t + k, n_tp)
        first = pl.multiple_of(t * features + me_o * part, part)
        copy = remote(
            w_ref.at[pl.ds(first, part), :], wbuf.at[me_t, rows_of(me_g, me_s), :], zs.at[k], zr.at[k], tp=t
        )
        copy.start()
        waits.append(copy)
    for k in range(1, n_tp):
        t = lax.rem(me_t + k, n_tp)
        copy = remote(ss_ref, ssbuf.at[k], ss_s.at[k], ss_r.at[k], tp=t)
        copy.start()
        waits.append(copy)

    local.wait()
    own[...] = jnp.dot(x_ref[...], wbuf[me_t], preferred_element_type=jnp.float32)

    for k in range(1, n_tp):
        t = lax.rem(me_t + n_tp - k, n_tp)
        waits[k - 1].wait_recv()
        mine = wbuf.at[t, rows_of(me_g, me_s), :]
        for j in range(1, n_seq):
            copy = remote(mine, mine, ps.at[k, j], pr.at[k, j], seq=lax.rem(me_s + j, n_seq))
            copy.start()
            waits.append(copy)
        for c in range(1, n_grp):
            copy = remote(mine, mine, gs.at[k, 0, c], gr.at[k, 0, c], grp=lax.rem(me_g + c, n_grp))
            copy.start()
            waits.append(copy)
    sent = []
    for k in range(1, n_tp):
        t = lax.rem(me_t + n_tp - k, n_tp)
        first = len(waits)
        for j in range(1, n_seq):
            s = lax.rem(me_s + n_seq - j, n_seq)
            theirs = wbuf.at[t, rows_of(me_g, s), :]
            remote(theirs, theirs, ps.at[k, j], pr.at[k, j], seq=s).wait_recv()
            for c in range(1, n_grp):
                copy = remote(theirs, theirs, gs.at[k, j, c], gr.at[k, j, c], grp=lax.rem(me_g + c, n_grp))
                copy.start()
                waits.append(copy)
        for j in range(n_seq):
            s = lax.rem(me_s + n_seq - j, n_seq)
            for c in range(1, n_grp):
                g = lax.rem(me_g + n_grp - c, n_grp)
                theirs = wbuf.at[t, rows_of(g, s), :]
                remote(theirs, theirs, gs.at[k, j, c], gr.at[k, j, c], grp=g).wait_recv()
        pbuf[k] = jnp.dot(x_ref[...], wbuf[t], preferred_element_type=jnp.float32).astype(jnp.bfloat16)
        copy = remote(pbuf.at[k], rbuf.at[k], ds.at[k], dr.at[k], tp=t)
        copy.start()
        sent.append(copy)

    total = ss_ref[...]
    for k in range(1, n_tp):
        waits[n_tp - 1 + k - 1].wait_recv()
        total = total + ssbuf[k]
    sstot[...] = total
    for k in range(1, n_tp):
        sent[k - 1].wait_recv()
    acc = own[...]
    for k in range(1, n_tp):
        acc = acc + rbuf[k].astype(jnp.float32)
    kvbuf[...] = acc.astype(jnp.bfloat16)

    out = []
    sub = lax.broadcasted_iota(jnp.int32, (8, 128), 0)
    for j in range(owners):
        o = lax.rem(me_o + j, owners)
        stage[j] = jnp.dot(
            pick_ref[j * GT : (j + 1) * GT], kvbuf[...], preferred_element_type=jnp.float32
        ).astype(jnp.bfloat16)
        sums = match_ref[j, 0] * sstot[0:1, :]
        for i in range(1, groups):
            sums = sums + match_ref[j, i] * sstot[i : i + 1, :]
        mstage[j] = jnp.where(sub == 0, jnp.broadcast_to(sums, (8, 128)), rows_ref[j])
        if j > 0:
            where = dict(grp=o // n_seq, seq=lax.rem(o, n_seq))
            for copy in (
                remote(stage.at[j], kland.at[j], ks.at[j], kr.at[j], **where),
                remote(mstage.at[j], mland.at[j], ms.at[j], mr.at[j], **where),
            ):
                copy.start()
                out.append(copy)
    akv_ref[0] = stage[0]
    ameta_ref[0] = mstage[0]
    for copy in out:
        copy.wait_recv()
    for j in range(1, owners):
        akv_ref[j] = kland[j]
        ameta_ref[j] = mland[j]
    for copy in waits + sent + out:
        copy.wait_send()


def output_kernel(
    n_seq, n_tp, attn_ref, w_ref, out_ref, wv, held, pbuf, rbuf, local_sem, as_, ar, ds, dr
):
    me_s, me_t = lax.axis_index("seq"), lax.axis_index("tp")
    per = n_seq // n_tp
    rows, columns = attn_ref.shape[0], w_ref.shape[1]
    tile = min(512, columns)
    local = pltpu.make_async_copy(w_ref, wv, local_sem)
    local.start()
    barrier = pltpu.get_barrier_semaphore()
    for k in range(1, n_tp):
        pl.semaphore_signal(barrier, inc=1, device_id={"tp": lax.rem(me_t + k, n_tp)}, device_id_type=MESH)
    for j in range(1, n_seq):
        pl.semaphore_signal(barrier, inc=1, device_id={"seq": lax.rem(me_s + j, n_seq)}, device_id_type=MESH)
    pl.semaphore_wait(barrier, n_tp - 1 + n_seq - 1)

    gathers = []
    for j in range(1, n_seq):
        copy = remote(attn_ref, held.at[j], as_.at[j], ar.at[j], seq=lax.rem(me_s + j, n_seq))
        copy.start()
        gathers.append(copy)
    local.wait()
    for j in range(n_seq):
        s = lax.rem(me_s + n_seq - j, n_seq)
        dest, sub = s // per, lax.rem(s, per)
        if j > 0:
            gathers[j - 1].wait_recv()
        block = attn_ref if j == 0 else held.at[j]

        @pl.loop(0, columns // tile)
        def _(c):
            cols = pl.ds(pl.multiple_of(c * tile, tile), tile)
            pbuf[s, :, cols] = jnp.dot(
                block[...], wv[:, cols], preferred_element_type=jnp.float32
            ).astype(jnp.bfloat16)

        @pl.when(dest != me_t)
        def _():
            remote(pbuf.at[s], rbuf.at[me_t, sub], ds.at[s], dr.at[me_t, sub], tp=dest).start()

    acc = [
        pbuf[pl.ds(me_t * per + u, 1)][0].astype(jnp.float32) for u in range(per)
    ]
    for k in range(1, n_tp):
        t = lax.rem(me_t + k, n_tp)
        for u in range(per):
            remote(pbuf.at[0], rbuf.at[t, u], ds.at[0], dr.at[t, u], tp=t).wait_recv()
            acc[u] = acc[u] + rbuf[pl.ds(t, 1), u][0].astype(jnp.float32)
    for u in range(per):
        out_ref[pl.ds(u * rows, rows), :] = acc[u].astype(jnp.bfloat16)
    for copy in gathers:
        copy.wait_send()
    for k in range(1, n_tp):
        t = lax.rem(me_t + k, n_tp)
        for u in range(per):
            s = t * per + u
            remote(pbuf.at[s], rbuf.at[me_t, u], ds.at[s], dr.at[me_t, u], tp=t).wait_send()


def on_device(
    prompt, w_kv, block_owner, block_row, queries, new_kv, cache_codes, cache_scales, lengths, w_out
):
    n_grp, n_seq, n_tp = lax.axis_size("grp"), lax.axis_size("seq"), lax.axis_size("tp")
    owners = n_grp * n_seq
    tokens, features = prompt.shape
    columns = w_kv.shape[1]
    row_count = queries.shape[0]
    groups = tokens // GT

    group_owner = block_owner[:, 0].reshape(groups, CAP)[:, 0]
    group_row = block_row.reshape(groups, CAP)[:, 0]
    me_o = lax.axis_index("grp") * n_seq + lax.axis_index("seq")
    order = (me_o + jnp.arange(owners, dtype=jnp.int32)) % owners
    match = group_owner[None, :] == order[:, None]
    token_of = jnp.arange(owners * GT)[:, None] % GT == jnp.arange(tokens)[None, :] % GT
    pick = jnp.repeat(jnp.repeat(match, GT, axis=0), GT, axis=1) & token_of
    send_row = jnp.sum(jnp.where(match, group_row[None, :] + 1, 0), axis=1) - 1
    row_tiles = jnp.broadcast_to(send_row.astype(jnp.float32)[:, None, None], (owners, 8, 128))
    widened = prompt.astype(jnp.float32)
    squares = jnp.sum(widened * widened, axis=1).reshape(groups, GT)
    squares = jnp.pad(squares, ((0, -groups % 8), (0, 128 - GT)))

    dma = pltpu.SemaphoreType.DMA
    vmem = pl.BlockSpec(memory_space=pltpu.VMEM)
    bf16, f32 = jnp.bfloat16, jnp.float32
    arrived, meta = pl.pallas_call(
        functools.partial(project_kernel, n_grp, n_seq, n_tp),
        out_shape=(
            jax.ShapeDtypeStruct((owners, GT, columns), bf16),
            jax.ShapeDtypeStruct((owners, 8, 128), f32),
        ),
        in_specs=[
            pl.BlockSpec(memory_space=pltpu.SMEM), vmem, pl.BlockSpec(memory_space=pl.ANY), vmem, vmem, vmem,
        ],
        out_specs=(vmem, vmem),
        scratch_shapes=[
            pltpu.VMEM((n_tp, features, columns), bf16),
            pltpu.VMEM((tokens, columns), f32),
            pltpu.VMEM((n_tp, tokens, columns), bf16),
            pltpu.VMEM((n_tp, tokens, columns), bf16),
            pltpu.VMEM((n_tp,) + squares.shape, f32),
            pltpu.VMEM(squares.shape, f32),
            pltpu.VMEM((tokens, columns), bf16),
            pltpu.VMEM((owners, GT, columns), bf16),
            pltpu.VMEM((owners, 8, 128), f32),
            pltpu.VMEM((owners, GT, columns), bf16),
            pltpu.VMEM((owners, 8, 128), f32),
            dma, dma((n_tp,)), dma((n_tp,)),
            dma((n_tp, n_seq)), dma((n_tp, n_seq)),
            dma((n_tp, n_seq, n_grp)), dma((n_tp, n_seq, n_grp)),
            dma((n_tp,)), dma((n_tp,)), dma((n_tp,)), dma((n_tp,)),
            dma((owners,)), dma((owners,)), dma((owners,)), dma((owners,)),
        ],
        compiler_params=pltpu.CompilerParams(
            collective_id=0, has_side_effects=True, vmem_limit_bytes=48 * MIB
        ),
        cost_estimate=pl.CostEstimate(
            flops=2 * tokens * features * columns * n_tp, bytes_accessed=16 * MIB, transcendentals=0
        ),
    )(match.astype(f32), prompt, w_kv, squares, row_tiles, pick.astype(bf16))

    kv_heads = columns // (2 * HD)
    head_group = HQ // KVH
    context = cache_codes.shape[1]
    query_heads = queries.reshape(row_count, NEW, kv_heads, head_group, HD)
    fresh_kv = new_kv.reshape(row_count, NEW, kv_heads, 2, HD)
    stored = cache_codes.reshape(row_count, context, kv_heads, 2, HD)
    block_scales = cache_scales.reshape(row_count, context // CBLK, kv_heads, 2)
    key_scale = jnp.transpose(jnp.repeat(block_scales[:, :, :, 0], CBLK, axis=1), (0, 2, 1))
    value_scale = jnp.transpose(jnp.repeat(block_scales[:, :, :, 1], CBLK, axis=1), (0, 2, 1))
    sent_kv = arrived.reshape(owners * GT, kv_heads, 2, HD)
    sent_rms = lax.rsqrt(meta[:, 0, :GT].reshape(owners * GT) / (features * n_tp) + EPS)
    sent_rows = jnp.repeat(meta[:, 1, 0].astype(jnp.int32), GT)
    inverse_root = 1.0 / math.sqrt(HD)
    row_ids = jnp.arange(row_count, dtype=jnp.int32)
    s_cache = jnp.einsum(
        "rinhd,rpnd->rinhp", query_heads, stored[:, :, :, 0, :], preferred_element_type=jnp.float32
    )
    s_cache = s_cache * key_scale[:, None, :, None, :] * inverse_root
    cache_live = jnp.arange(context, dtype=jnp.int32)[None, :] < lengths[:, None]
    s_cache = jnp.where(cache_live[:, None, None, None, :], s_cache, -jnp.inf)
    s_sent = (
        jnp.einsum(
            "rinhd,knd->rinhk", query_heads, sent_kv[:, :, 0, :], preferred_element_type=jnp.float32
        )
        * sent_rms
        * inverse_root
    )
    sent_live = sent_rows[None, :] == row_ids[:, None]
    s_sent = jnp.where(sent_live[:, None, None, None, :], s_sent, -jnp.inf)
    s_fresh = (
        jnp.einsum(
            "rinhd,rjnd->rinhj",
            query_heads,
            fresh_kv[:, :, :, 0, :],
            preferred_element_type=jnp.float32,
        )
        * inverse_root
    )
    causal = jnp.arange(NEW)[None, :] <= jnp.arange(NEW)[:, None]
    s_fresh = jnp.where(causal[None, :, None, None, :], s_fresh, -jnp.inf)
    row_max = jnp.maximum(
        jnp.maximum(jnp.max(s_cache, axis=-1), jnp.max(s_sent, axis=-1)), jnp.max(s_fresh, axis=-1)
    )
    w_cache = jnp.exp(s_cache - row_max[..., None])
    w_sent = jnp.exp(s_sent - row_max[..., None])
    w_fresh = jnp.exp(s_fresh - row_max[..., None])
    denominator = jnp.sum(w_cache, axis=-1) + jnp.sum(w_sent, axis=-1) + jnp.sum(w_fresh, axis=-1)
    cache_weights = (w_cache * value_scale[:, None, :, None, :]).astype(jnp.bfloat16)
    numerator = jnp.einsum(
        "rinhp,rpnd->rinhd",
        cache_weights,
        stored[:, :, :, 1, :],
        preferred_element_type=jnp.float32,
    )
    numerator = numerator + jnp.einsum(
        "rinhk,knd->rinhd",
        (w_sent * sent_rms).astype(jnp.bfloat16),
        sent_kv[:, :, 1, :],
        preferred_element_type=jnp.float32,
    )
    numerator = numerator + jnp.einsum(
        "rinhj,rjnd->rinhd",
        w_fresh.astype(jnp.bfloat16),
        fresh_kv[:, :, :, 1, :],
        preferred_element_type=jnp.float32,
    )
    attention = (
        (numerator / denominator[..., None])
        .astype(jnp.bfloat16)
        .reshape(row_count * NEW, kv_heads * head_group * HD)
    )
    rows, depth = attention.shape
    per = n_seq // n_tp
    out_columns = w_out.shape[1]
    return pl.pallas_call(
        functools.partial(output_kernel, n_seq, n_tp),
        out_shape=jax.ShapeDtypeStruct((per * rows, out_columns), bf16),
        in_specs=[vmem, pl.BlockSpec(memory_space=pl.ANY)],
        out_specs=vmem,
        scratch_shapes=[
            pltpu.VMEM((depth, out_columns), bf16),
            pltpu.VMEM((n_seq, rows, depth), bf16),
            pltpu.VMEM((n_seq, rows, out_columns), bf16),
            pltpu.VMEM((n_tp, per, rows, out_columns), bf16),
            dma, dma((n_seq,)), dma((n_seq,)), dma((n_seq,)), dma((n_tp, per)),
        ],
        compiler_params=pltpu.CompilerParams(
            collective_id=1, has_side_effects=True, vmem_limit_bytes=48 * MIB
        ),
        cost_estimate=pl.CostEstimate(
            flops=2 * rows * n_seq * depth * out_columns, bytes_accessed=16 * MIB, transcendentals=0
        ),
    )(attention, w_out)


def solution(mesh):
    in_specs = (
        P(("grp", "seq"), "tp"),
        P(None, "tp"),
        P(("grp", "seq"), None),
        P(("grp", "seq")),
        P(("grp", "seq"), None, "tp"),
        P(("grp", "seq"), None, "tp"),
        P(("grp", "seq"), None, "tp"),
        P(("grp", "seq"), None, "tp"),
        P(("grp", "seq")),
        P("tp", "seq"),
    )
    out_specs = P(("grp", "tp"), "seq")
    return jax.shard_map(
        on_device, mesh=mesh, in_specs=in_specs, out_specs=out_specs, check_vma=False
    )
```

time: 297 us -> 202 us (0.68)
  waiting for transfers between devices: 214 us -> 0 us
  Pallas kernels: 0 us -> 160 us
  matrix products: 31.5 us -> 16.1 us
  between operations: 13.4 us -> 0.24 us
  starting transfers between devices: 8.44 us -> 0 us
  other arithmetic: 13.5 us -> 9.88 us
    all_gather x2 -> x0, waiting for transfers between devices: 165 us -> none  [the longest x1 133 us: on_device(): shard_piece = lax.all_gather(prompt, 'tp', axis=1, tiled=True)]
    pallas_call x0 -> x2, Pallas kernels: none -> 160 us  [the longest x1 94.6 us: on_device(): pl.pallas_call(functools.partial(project_kernel, n_grp, n_seq, n_tp), out...]
    reduce_scatter x1 -> x0, waiting for transfers between devices: 44.9 us -> none  [on_device(): lax.psum_scatter(head_terms.astype(jnp.bfloat16), 'tp', scatter_dimension...]
    dot_general x5 -> x2, matrix products: 23.3 us -> 6.61 us  [the longest x1 3.45 us: on_device(): jnp.einsum('rinhk,knd->rinhd', (w_sent * sent_rms).astype(jnp.bfloat16),...]
    all_to_all x2 -> x0, starting transfers between devices: 8.4 us -> none  [the longest x1 4.2 us: on_device(): lax.all_to_all(send_kv, ('grp', 'seq'), split_axis=0, concat_axis=0, tile...]
    reduce_sum x3 -> x2, other arithmetic: 6.2 us -> 2.26 us  [the longest x1 2.08 us: on_device(): squares = jnp.sum(widened * widened, axis=1).reshape(groups, GT)]
    all_to_all x2 -> x0, waiting for transfers between devices: 3.23 us -> none  [the longest x1 3.22 us: on_device(): lax.all_to_all(send_kv, ('grp', 'seq'), split_axis=0, concat_axis=0, tile...]
    unnamed x13 -> x17, local copies, waits for them, and re-layouts: 7.3 us -> 9.54 us
  transfers between devices with their start and end apart: 5 -> 0, of which waited for: 4 -> 0; matrix products, arithmetic and copies ran while one was open for 11% -> 0% of each run, Pallas kernels for 0% -> 0%
where the time goes in v1:
time: 202 us; the launch traced here: 201 us
  Pallas kernels  160 us (79%)
  matrix products  16.1 us (8%)
  local copies, waits for them, and re-layouts  15.2 us (8%)
  other arithmetic  9.88 us (5%)
    pallas_call x1, Pallas kernels, on_device(): pl.pallas_call(functools.partial(project_kernel, n_grp, n_seq, n_tp), out...  94.6 us
    pallas_call x1, Pallas kernels, on_device(): pl.pallas_call(functools.partial(output_kernel, n_seq, n_tp), out_shape=j...  65.3 us
    unnamed x17, local copies, waits for them, and re-layouts  9.54 us

profile of v1, /device:TPU:6, one launch (start us, length us, event | category | flops | bytes accessed | tf_op | source)
XLA Modules:
  0.0 201.2 jit_solution(18124465912931783672)
XLA Ops:
  0.0 0.5 broadcast.162
  0.5 1.3 reduce.13
  1.8 0.1 reshape_squeeze.4
  1.9 0.7 reshape.180
  2.7 0.1 add_reduce_fusion
  2.8 0.1 broadcast_compare_fusion
  2.9 0.1 copy.68
  3.0 0.1 broadcast_in_dim.94
  3.1 0.1 reshape.181
  3.2 0.1 broadcast_in_dim.95
  3.2 0.4 copy.69
  3.6 0.3 and_convert_fusion.pick_ref
  3.9 0.2 select_reduce_fusion
  4.1 0.1 broadcast_in_dim.93.rows_ref
  4.2 2.1 %multiply_reduce_fusion = f32[512]{0:T(512)S(1)} fusion(bf16[512,2048]{1,0:T(8,128)(2,1)} %x_ref.1), kind=kLoop, calls=%fused_computation.3 | loop fusion | flops 3145216 | bytes 2099200 | tf_op jit(solution)/shard_map/reduce_sum | solution.py:237
  6.3 0.1 reshape.179
  6.3 0.0 copy-start
  6.3 1.6 copy-done
  7.9 0.0 copy-start.2
  7.9 94.6 %shard_map.100 = (bf16[8,64,512]{2,1,0:T(8,128)(2,1)S(1)}, f32[8,8,128]{2,1,0:T(8,128)S(1)}) custom-call(f32[8,8]{1,0:T(8,128)S(1)} %get-tuple-element.18.match_ref, bf16[512,2048]{1,0:T(8,128)(2,1)S(1)} %copy-done, bf16[8192,512]{1,0:T(8,128)(2,1)} %w_ref.2, f32[8,128]{1,0:T(8,128)S(1)} %pad.4.ss_ref, f32[8,8,128]{2,1,0:T(8,128)S(1)} %broadcast_in_dim.93.rows_ref, ...), custom_call_target="tpu_custom_call" | custom-call | flops 4294967296 | bytes 16777216 | tf_op jit(solution)/shard_map/pallas_call | solution.py:243
  102.5 0.2 convert_reduce_fusion
  102.8 0.1 broadcast_in_dim.96
  102.8 0.1 eq.60
  103.0 0.1 rsqrt.11
  103.1 0.1 reshape.183
  103.2 1.5 fusion.35
  104.7 0.0 copy-done.2
  104.7 0.3 reshape.176
  105.0 3.2 %fusion.1 = (f32[32,4,2,8]{0,3,1,2:T(8,128)S(1)}, f32[2,512,32,4,8]{1,2,4,3,0:T(8,128)}) fusion(f32[512]{0:T(512)S(1)} %rsqrt.11, pred[32,512]{1,0:T(8,128)(4,1)S(1)} %iota_compare_fusion, bf16[32,4,2,8,128]{4,3,2,1,0:T(8,128)(2,1)S(1)} %reshape.176, bf16[512,2,1,128]{3,2,1,0:T(2,128)(2,1)S(1)} %get-tuple-element.12), kind=kOutput, calls=%fused_computation.5 | convolution fusion | flops 272627712 | bytes 5007360 | tf_op jit(solution)/shard_map/rinhd,knd->rinhk/dot_general | solution.py:300
  108.2 0.1 copy.72
  108.3 0.0 copy-start.5
  108.3 0.0 copy-start.6
  108.4 6.6 %copy.63 = bf16[32,128,512]{1,2,0:T(8,128)(2,1)} copy(bf16[32,128,512]{2,1,0:T(8,128)(2,1)} %param.16) | data formatting | bytes 8388608 | tf_op args[6]
  115.0 0.0 copy-start.3
  115.0 0.0 copy-done.5
  115.0 0.1 copy.67
  115.1 0.0 copy-done.6
  115.1 0.1 iota_compare_fusion.1
  115.2 2.4 %fusion.39 = (f32[32,4,2,8]{3,1,2,0:T(4,128)S(1)}, f32[32,4,2,8,128]{4,3,1,2,0:T(8,128)S(1)}) fusion(f32[32,2,128]{2,1,0:T(2,128)S(1)} %copy.67, bf16[32,4,2,8,128]{4,3,2,1,0:T(8,128)(2,1)S(1)} %reshape.176, bf16[32,128,2,2,128]{1,4,3,2,0:T(8,128)(2,1)} %bitcast.110, pred[32,128]{1,0:T(8,128)(4,1)S(1)} %iota_compare_fusion.1), kind=kOutput, calls=%fused_computation.70 | convolution fusion | flops 68155392 | bytes 3715072 | tf_op jit(solution)/shard_map/rinhd,rpnd->rinhp/dot_general | solution.py:293
  117.6 0.0 copy-done.3
  117.6 0.1 reshape.193
  117.6 0.8 fusion.36
  118.5 3.3 %fusion.38 = (f32[32,4,2,8]{3,1,2,0:T(4,128)S(1)}, f32[32,4,2,8,4]{3,4,1,2,0:T(4,128)}) fusion(bf16[32,4,2,8,128]{4,3,2,1,0:T(8,128)(2,1)S(1)} %reshape.176, bf16[32,4,2,1,128]{4,3,2,1,0:T(2,128)(2,1)S(1)} %get-tuple-element.14, pred[4,4]{1,0:T(4,128)(4,1)S(1)} %iota_compare_fusion.2), kind=kOutput, calls=%fused_computation.69 | convolution fusion | flops 2119680 | bytes 630800 | tf_op jit(solution)/shard_map/rinhd,rjnd->rinhj/dot_general | solution.py:309
  121.8 0.1 copy.80
  121.9 3.1 %fusion = (f32[32,4,2,8]{0,3,1,2:T(8,128)S(1)}, bf16[32,4,2,8,512]{4,0,3,1,2:T(8,128)(2,1)S(1)}) fusion(f32[2,512,32,4,8]{1,2,4,3,0:T(8,128)} %get-tuple-element.24, f32[32,4,2,8]{0,3,1,2:T(8,128)S(1)} %copy.80, f32[512]{0:T(512)S(1)} %rsqrt.11, pred[32,512]{1,0:T(8,128)(4,1)S(1)} %iota_compare_fusion), kind=kLoop, calls=%fused_computation.4 | loop fusion | flops 7337984 | bytes 6326272 | tf_op jit(solution)/shard_map/reduce_sum | solution.py:325
  125.0 0.1 copy.83
  125.1 0.8 fusion.20
  125.9 1.5 fusion.27
  127.5 3.4 %fusion.7 = f32[32,4,2,8,128]{4,3,1,2,0:T(8,128)} fusion(bf16[32,4,2,8,512]{4,0,3,1,2:T(8,128)(2,1)S(1)} %get-tuple-element.10, bf16[512,2,1,128]{3,2,1,0:T(2,128)(2,1)} %get-tuple-element.11), kind=kOutput, calls=%fused_computation.13 | convolution fusion | flops 268435456 | bytes 3407872 | tf_op jit(solution)/shard_map/rinhk,knd->rinhd/dot_general | solution.py:333
  130.9 0.0 copy-start.1
  130.9 0.0 copy-start.4
  130.9 0.1 copy.77
  131.0 3.2 %fusion.12 = f32[32,4,2,8,128]{4,3,1,2,0:T(8,128)S(1)} fusion(f32[32,4,2,8,128]{4,3,1,2,0:T(8,128)} %fusion.7, bf16[32,128,2,2,128]{1,4,3,2,0:T(8,128)(2,1)} %bitcast.111, f32[32,4,2,8,128]{4,3,1,2,0:T(8,128)S(1)} %get-tuple-element.22, f32[32,2,128]{2,1,0:T(2,128)S(1)} %copy.77, f32[32,4,2,8]{3,1,2,0:T(4,128)S(1)} %bitcast.115), kind=kOutput, calls=%fused_computation.17 | convolution fusion | flops 68157440 | bytes 5283840 | tf_op jit(solution)/shard_map/rinhp,rpnd->rinhd/dot_general | solution.py:327
  134.2 0.0 copy-done.1
  134.2 0.0 copy-done.4
  134.2 0.6 fusion.17
  134.8 0.1 copy.84
  134.9 0.2 reshape.186.attn_ref
  135.2 65.3 %shard_map.101 = bf16[128,2048]{1,0:T(8,128)(2,1)S(1)} custom-call(bf16[128,2048]{1,0:T(8,128)(2,1)S(1)} %reshape.186.attn_ref, bf16[2048,2048]{1,0:T(8,128)(2,1)} %w_ref.3), custom_call_target="tpu_custom_call" | custom-call | flops 4294967296 | bytes 16777216 | tf_op jit(solution)/shard_map/pallas_call | solution.py:353
  200.5 0.8 copy.129
  (14 shorter events, 0.2 us)
Async XLA Ops:
  6.3 1.6 copy-start
  7.9 96.8 %copy-start.2 = (bf16[32,4,2048]{2,1,0:T(4,128)(2,1)S(1)}, bf16[32,4,2048]{2,1,0:T(4,128)(2,1)}, u32[]{:S(2)}) copy-start(bf16[32,4,2048]{2,1,0:T(4,128)(2,1)} %param.14) | copy-start | bytes 1572868
  108.3 6.6 %copy-start.5 = (f32[32,8,4]{0,2,1:T(4,128)S(1)}, f32[32,8,4]{0,2,1:T(4,128)}, u32[]{:S(2)}) copy-start(f32[32,8,4]{0,2,1:T(4,128)} %param.17) | copy-start | bytes 12292
  108.3 6.7 %copy-start.6 = (s32[32]{0:T(128)S(1)}, s32[32]{0:T(128)}, u32[]{:S(2)}) copy-start(s32[32]{0:T(128)} %param.18) | copy-start | bytes 388
  115.0 2.6 %copy-start.3 = (bf16[32,4,512]{2,1,0:T(4,128)(2,1)S(1)}, bf16[32,4,512]{2,1,0:T(4,128)(2,1)}, u32[]{:S(2)}) copy-start(bf16[32,4,512]{2,1,0:T(4,128)(2,1)} %param.15) | copy-start | bytes 393220
  130.9 3.3 %copy-start.1 = (f32[32,4,2,8,4]{3,4,1,2,0:T(4,128)S(1)}, f32[32,4,2,8,4]{3,4,1,2,0:T(4,128)}, u32[]{:S(2)}) copy-start(f32[32,4,2,8,4]{3,4,1,2,0:T(4,128)} %get-tuple-element.20) | copy-start | bytes 98308
  130.9 3.3 %copy-start.4 = (bf16[32,4,2,1,128]{4,3,2,1,0:T(2,128)(2,1)S(1)}, bf16[32,4,2,1,128]{4,3,2,1,0:T(2,128)(2,1)}, u32[]{:S(2)}) copy-start(bf16[32,4,2,1,128]{4,3,2,1,0:T(2,128)(2,1)} %get-tuple-element.13) | copy-start | bytes 196612

commit v2 on v1

--- a/solution.py
+++ b/solution.py
@@ -41,6 +41,9 @@
     features = x_ref.shape[1]
     part = features // owners
     groups = x_ref.shape[0] // GT
+    width = rbuf.shape[-1]
+    chunks = w_ref.shape[1] // width
+    cols = [slice(c * width, (c + 1) * width) for c in range(chunks)]
     waits = []
 
     def rows_of(g, s):
@@ -61,69 +64,88 @@
         )
     pl.semaphore_wait(barrier, n_tp - 1 + owners - 1)
 
-    for k in range(1, n_tp):
-        t = lax.rem(me_t + k, n_tp)
-        first = pl.multiple_of(t * features + me_o * part, part)
-        copy = remote(
-            w_ref.at[pl.ds(first, part), :], wbuf.at[me_t, rows_of(me_g, me_s), :], zs.at[k], zr.at[k], tp=t
-        )
+    def w_sends(c):
+        copies = []
+        for k in range(1, n_tp):
+            t = lax.rem(me_t + k, n_tp)
+            first = pl.multiple_of(t * features + me_o * part, part)
+            copies.append(remote(
+                w_ref.at[pl.ds(first, part), cols[c]], wbuf.at[me_t, rows_of(me_g, me_s), cols[c]],
+                zs.at[c, k], zr.at[c, k], tp=t,
+            ))
+            copies[-1].start()
+        return copies
+
+    w_copies = [w_sends(0)]
+    ss_copies = []
+    for k in range(1, n_tp):
+        copy = remote(ss_ref, ssbuf.at[k], ss_s.at[k], ss_r.at[k], tp=lax.rem(me_t + k, n_tp))
         copy.start()
-        waits.append(copy)
-    for k in range(1, n_tp):
-        t = lax.rem(me_t + k, n_tp)
-        copy = remote(ss_ref, ssbuf.at[k], ss_s.at[k], ss_r.at[k], tp=t)
-        copy.start()
-        waits.append(copy)
+        ss_copies.append(copy)
 
     local.wait()
     own[...] = jnp.dot(x_ref[...], wbuf[me_t], preferred_element_type=jnp.float32)
-
-    for k in range(1, n_tp):
-        t = lax.rem(me_t + n_tp - k, n_tp)
-        waits[k - 1].wait_recv()
-        mine = wbuf.at[t, rows_of(me_g, me_s), :]
-        for j in range(1, n_seq):
-            copy = remote(mine, mine, ps.at[k, j], pr.at[k, j], seq=lax.rem(me_s + j, n_seq))
-            copy.start()
-            waits.append(copy)
-        for c in range(1, n_grp):
-            copy = remote(mine, mine, gs.at[k, 0, c], gr.at[k, 0, c], grp=lax.rem(me_g + c, n_grp))
-            copy.start()
-            waits.append(copy)
-    sent = []
-    for k in range(1, n_tp):
-        t = lax.rem(me_t + n_tp - k, n_tp)
-        first = len(waits)
-        for j in range(1, n_seq):
-            s = lax.rem(me_s + n_seq - j, n_seq)
-            theirs = wbuf.at[t, rows_of(me_g, s), :]
-            remote(theirs, theirs, ps.at[k, j], pr.at[k, j], seq=s).wait_recv()
-            for c in range(1, n_grp):
-                copy = remote(theirs, theirs, gs.at[k, j, c], gr.at[k, j, c], grp=lax.rem(me_g + c, n_grp))
+    for c in range(1, chunks):
+        for copy in w_copies[c - 1]:
+            copy.wait_send()
+        w_copies.append(w_sends(c))
+    for copy in w_copies[-1]:
+        waits.append(copy)
+    waits.extend(ss_copies)
+
+    for c in range(chunks):
+        for k in range(1, n_tp):
+            t = lax.rem(me_t + n_tp - k, n_tp)
+            w_copies[c][k - 1].wait_recv()
+            mine = wbuf.at[t, rows_of(me_g, me_s), cols[c]]
+            for j in range(1, n_seq):
+                copy = remote(mine, mine, ps.at[c, k, j], pr.at[c, k, j], seq=lax.rem(me_s + j, n_seq))
                 copy.start()
                 waits.append(copy)
-        for j in range(n_seq):
-            s = lax.rem(me_s + n_seq - j, n_seq)
-            for c in range(1, n_grp):
-                g = lax.rem(me_g + n_grp - c, n_grp)
-                theirs = wbuf.at[t, rows_of(g, s), :]
-                remote(theirs, theirs, gs.at[k, j, c], gr.at[k, j, c], grp=g).wait_recv()
-        pbuf[k] = jnp.dot(x_ref[...], wbuf[t], preferred_element_type=jnp.float32).astype(jnp.bfloat16)
-        copy = remote(pbuf.at[k], rbuf.at[k], ds.at[k], dr.at[k], tp=t)
-        copy.start()
-        sent.append(copy)
+            for e in range(1, n_grp):
+                copy = remote(mine, mine, gs.at[c, k, 0, e], gr.at[c, k, 0, e], grp=lax.rem(me_g + e, n_grp))
+                copy.start()
+                waits.append(copy)
+    sent = []
+    for c in range(chunks):
+        for k in range(1, n_tp):
+            t = lax.rem(me_t + n_tp - k, n_tp)
+            for j in range(1, n_seq):
+                s = lax.rem(me_s + n_seq - j, n_seq)
+                theirs = wbuf.at[t, rows_of(me_g, s), cols[c]]
+                remote(theirs, theirs, ps.at[c, k, j], pr.at[c, k, j], seq=s).wait_recv()
+                for e in range(1, n_grp):
+                    copy = remote(
+                        theirs, theirs, gs.at[c, k, j, e], gr.at[c, k, j, e], grp=lax.rem(me_g + e, n_grp)
+                    )
+                    copy.start()
+                    waits.append(copy)
+        for k in range(1, n_tp):
+            t = lax.rem(me_t + n_tp - k, n_tp)
+            for j in range(n_seq):
+                s = lax.rem(me_s + n_seq - j, n_seq)
+                for e in range(1, n_grp):
+                    g = lax.rem(me_g + n_grp - e, n_grp)
+                    theirs = wbuf.at[t, rows_of(g, s), cols[c]]
+                    remote(theirs, theirs, gs.at[c, k, j, e], gr.at[c, k, j, e], grp=g).wait_recv()
+            pbuf[k, c] = jnp.dot(
+                x_ref[...], wbuf[t, :, cols[c]], preferred_element_type=jnp.float32
+            ).astype(jnp.bfloat16)
+            copy = remote(pbuf.at[k, c], rbuf.at[k, c], ds.at[c, k], dr.at[c, k], tp=t)
+            copy.start()
+            sent.append(copy)
 
     total = ss_ref[...]
     for k in range(1, n_tp):
-        waits[n_tp - 1 + k - 1].wait_recv()
+        ss_copies[k - 1].wait_recv()
         total = total + ssbuf[k]
     sstot[...] = total
-    for k in range(1, n_tp):
-        sent[k - 1].wait_recv()
-    acc = own[...]
-    for k in range(1, n_tp):
-        acc = acc + rbuf[k].astype(jnp.float32)
-    kvbuf[...] = acc.astype(jnp.bfloat16)
+    for c in range(chunks):
+        acc = own[:, cols[c]]
+        for k in range(1, n_tp):
+            sent[c * (n_tp - 1) + k - 1].wait_recv()
+            acc = acc + rbuf[k, c].astype(jnp.float32)
+        kvbuf[:, cols[c]] = acc.astype(jnp.bfloat16)
 
     out = []
     sub = lax.broadcasted_iota(jnp.int32, (8, 128), 0)
@@ -155,6 +177,61 @@
         copy.wait_send()
 
 
+def attention_kernel(
+    kv_heads, head_group, inverse_root,
+    lengths_ref, q_ref, new_ref, cache_ref, scale_ref, sent_ref, rms_ref, rows_ref, out_ref,
+):
+    f32, bf16 = jnp.float32, jnp.bfloat16
+    step_rows, context = cache_ref.shape[0], cache_ref.shape[1]
+    head_rows = head_group * NEW
+    all_rows = step_rows * head_rows
+    first = pl.program_id(0) * step_rows
+    position = lax.broadcasted_iota(jnp.int32, (head_rows, context), 1)
+
+    def scores(a, b):
+        return lax.dot_general(a, b, (((1,), (1,)), ((), ())), preferred_element_type=f32)
+
+    sent_count, new_count = sent_ref.shape[0], step_rows * NEW
+    of_row = lax.broadcasted_iota(jnp.int32, (all_rows, sent_count), 0) // head_rows + first
+    sent_live = rows_ref[...] == of_row.astype(f32)
+    row = lax.broadcasted_iota(jnp.int32, (all_rows, new_count), 0)
+    column = lax.broadcasted_iota(jnp.int32, (all_rows, new_count), 1)
+    new_live = (column // NEW == row // head_rows) & (column % NEW <= row % NEW)
+    for n in range(kv_heads):
+        key = slice(n * 2 * HD, n * 2 * HD + HD)
+        value = slice(n * 2 * HD + HD, (n + 1) * 2 * HD)
+        q = q_ref[n]
+        parts = []
+        for r in range(step_rows):
+            part = scores(q[r * head_rows : (r + 1) * head_rows], cache_ref[r, :, key])
+            part = part * scale_ref[n, 0, r : r + 1, :] * inverse_root
+            parts.append(jnp.where(position < lengths_ref[first + r], part, -jnp.inf))
+        s_cache = jnp.concatenate(parts, axis=0)
+        s_sent = scores(q, sent_ref[:, key]) * rms_ref[...] * inverse_root
+        s_sent = jnp.where(sent_live, s_sent, -jnp.inf)
+        s_new = jnp.where(new_live, scores(q, new_ref[:, key]) * inverse_root, -jnp.inf)
+        top = jnp.maximum(
+            jnp.maximum(jnp.max(s_cache, axis=1, keepdims=True), jnp.max(s_sent, axis=1, keepdims=True)),
+            jnp.max(s_new, axis=1, keepdims=True),
+        )
+        w_cache, w_sent, w_new = jnp.exp(s_cache - top), jnp.exp(s_sent - top), jnp.exp(s_new - top)
+        denominator = (
+            jnp.sum(w_cache, axis=1, keepdims=True)
+            + jnp.sum(w_sent, axis=1, keepdims=True)
+            + jnp.sum(w_new, axis=1, keepdims=True)
+        )
+        parts = []
+        for r in range(step_rows):
+            part = w_cache[r * head_rows : (r + 1) * head_rows] * scale_ref[n, 1, r : r + 1, :]
+            parts.append(jnp.dot(part.astype(bf16), cache_ref[r, :, value], preferred_element_type=f32))
+        total = jnp.concatenate(parts, axis=0)
+        total = total + jnp.dot(
+            (w_sent * rms_ref[...]).astype(bf16), sent_ref[:, value], preferred_element_type=f32
+        )
+        total = total + jnp.dot(w_new.astype(bf16), new_ref[:, value], preferred_element_type=f32)
+        out_ref[n] = (total / denominator).astype(bf16)
+
+
 def output_kernel(
     n_seq, n_tp, attn_ref, w_ref, out_ref, wv, held, pbuf, rbuf, local_sem, as_, ar, ds, dr
 ):
@@ -237,6 +314,8 @@
     squares = jnp.sum(widened * widened, axis=1).reshape(groups, GT)
     squares = jnp.pad(squares, ((0, -groups % 8), (0, 128 - GT)))
 
+    width = min(256, columns)
+    chunks = columns // width
     dma = pltpu.SemaphoreType.DMA
     vmem = pl.BlockSpec(memory_space=pltpu.VMEM)
     bf16, f32 = jnp.bfloat16, jnp.float32
@@ -253,8 +332,8 @@
         scratch_shapes=[
             pltpu.VMEM((n_tp, features, columns), bf16),
             pltpu.VMEM((tokens, columns), f32),
-            pltpu.VMEM((n_tp, tokens, columns), bf16),
-            pltpu.VMEM((n_tp, tokens, columns), bf16),
+            pltpu.VMEM((n_tp, chunks, tokens, width), bf16),
+            pltpu.VMEM((n_tp, chunks, tokens, width), bf16),
             pltpu.VMEM((n_tp,) + squares.shape, f32),
             pltpu.VMEM(squares.shape, f32),
             pltpu.VMEM((tokens, columns), bf16),
@@ -262,10 +341,10 @@
             pltpu.VMEM((owners, 8, 128), f32),
             pltpu.VMEM((owners, GT, columns), bf16),
             pltpu.VMEM((owners, 8, 128), f32),
-            dma, dma((n_tp,)), dma((n_tp,)),
-            dma((n_tp, n_seq)), dma((n_tp, n_seq)),
-            dma((n_tp, n_seq, n_grp)), dma((n_tp, n_seq, n_grp)),
-            dma((n_tp,)), dma((n_tp,)), dma((n_tp,)), dma((n_tp,)),
+            dma, dma((chunks, n_tp)), dma((chunks, n_tp)),
+            dma((chunks, n_tp, n_seq)), dma((chunks, n_tp, n_seq)),
+            dma((chunks, n_tp, n_seq, n_grp)), dma((chunks, n_tp, n_seq, n_grp)),
+            dma((chunks, n_tp)), dma((chunks, n_tp)), dma((n_tp,)), dma((n_tp,)),
             dma((owners,)), dma((owners,)), dma((owners,)), dma((owners,)),
         ],
         compiler_params=pltpu.CompilerParams(
@@ -279,74 +358,45 @@
     kv_heads = columns // (2 * HD)
     head_group = HQ // KVH
     context = cache_codes.shape[1]
-    query_heads = queries.reshape(row_count, NEW, kv_heads, head_group, HD)
-    fresh_kv = new_kv.reshape(row_count, NEW, kv_heads, 2, HD)
-    stored = cache_codes.reshape(row_count, context, kv_heads, 2, HD)
-    block_scales = cache_scales.reshape(row_count, context // CBLK, kv_heads, 2)
-    key_scale = jnp.transpose(jnp.repeat(block_scales[:, :, :, 0], CBLK, axis=1), (0, 2, 1))
-    value_scale = jnp.transpose(jnp.repeat(block_scales[:, :, :, 1], CBLK, axis=1), (0, 2, 1))
-    sent_kv = arrived.reshape(owners * GT, kv_heads, 2, HD)
-    sent_rms = lax.rsqrt(meta[:, 0, :GT].reshape(owners * GT) / (features * n_tp) + EPS)
-    sent_rows = jnp.repeat(meta[:, 1, 0].astype(jnp.int32), GT)
     inverse_root = 1.0 / math.sqrt(HD)
-    row_ids = jnp.arange(row_count, dtype=jnp.int32)
-    s_cache = jnp.einsum(
-        "rinhd,rpnd->rinhp", query_heads, stored[:, :, :, 0, :], preferred_element_type=jnp.float32
-    )
-    s_cache = s_cache * key_scale[:, None, :, None, :] * inverse_root
-    cache_live = jnp.arange(context, dtype=jnp.int32)[None, :] < lengths[:, None]
-    s_cache = jnp.where(cache_live[:, None, None, None, :], s_cache, -jnp.inf)
-    s_sent = (
-        jnp.einsum(
-            "rinhd,knd->rinhk", query_heads, sent_kv[:, :, 0, :], preferred_element_type=jnp.float32
-        )
-        * sent_rms
-        * inverse_root
-    )
-    sent_live = sent_rows[None, :] == row_ids[:, None]
-    s_sent = jnp.where(sent_live[:, None, None, None, :], s_sent, -jnp.inf)
-    s_fresh = (
-        jnp.einsum(
-            "rinhd,rjnd->rinhj",
-            query_heads,
-            fresh_kv[:, :, :, 0, :],
-            preferred_element_type=jnp.float32,
-        )
-        * inverse_root
-    )
-    causal = jnp.arange(NEW)[None, :] <= jnp.arange(NEW)[:, None]
-    s_fresh = jnp.where(causal[None, :, None, None, :], s_fresh, -jnp.inf)
-    row_max = jnp.maximum(
-        jnp.maximum(jnp.max(s_cache, axis=-1), jnp.max(s_sent, axis=-1)), jnp.max(s_fresh, axis=-1)
-    )
-    w_cache = jnp.exp(s_cache - row_max[..., None])
-    w_sent = jnp.exp(s_sent - row_max[..., None])
-    w_fresh = jnp.exp(s_fresh - row_max[..., None])
-    denominator = jnp.sum(w_cache, axis=-1) + jnp.sum(w_sent, axis=-1) + jnp.sum(w_fresh, axis=-1)
-    cache_weights = (w_cache * value_scale[:, None, :, None, :]).astype(jnp.bfloat16)
-    numerator = jnp.einsum(
-        "rinhp,rpnd->rinhd",
-        cache_weights,
-        stored[:, :, :, 1, :],
-        preferred_element_type=jnp.float32,
-    )
-    numerator = numerator + jnp.einsum(
-        "rinhk,knd->rinhd",
-        (w_sent * sent_rms).astype(jnp.bfloat16),
-        sent_kv[:, :, 1, :],
-        preferred_element_type=jnp.float32,
-    )
-    numerator = numerator + jnp.einsum(
-        "rinhj,rjnd->rinhd",
-        w_fresh.astype(jnp.bfloat16),
-        fresh_kv[:, :, :, 1, :],
-        preferred_element_type=jnp.float32,
-    )
-    attention = (
-        (numerator / denominator[..., None])
-        .astype(jnp.bfloat16)
-        .reshape(row_count * NEW, kv_heads * head_group * HD)
-    )
+    head_rows = head_group * NEW
+    query_heads = jnp.transpose(
+        queries.reshape(row_count, NEW, kv_heads, head_group, HD), (2, 0, 3, 1, 4)
+    ).reshape(kv_heads, row_count * head_rows, HD)
+    block_scales = jnp.transpose(
+        cache_scales.reshape(row_count, context // CBLK, kv_heads, 2), (2, 3, 0, 1)
+    )
+    scales = jnp.repeat(block_scales, CBLK, axis=3)
+    sent_rms = lax.rsqrt(meta[:, 0, :GT].reshape(1, owners * GT) / (features * n_tp) + EPS)
+    sent_rows = jnp.repeat(meta[:, 1, 0], GT)[None, :]
+    step_rows = 8
+    attention = pl.pallas_call(
+        functools.partial(attention_kernel, kv_heads, head_group, inverse_root),
+        grid=(row_count // step_rows,),
+        out_shape=jax.ShapeDtypeStruct((kv_heads, row_count * head_rows, HD), bf16),
+        in_specs=[
+            pl.BlockSpec(memory_space=pltpu.SMEM),
+            pl.BlockSpec((kv_heads, step_rows * head_rows, HD), lambda i: (0, i, 0)),
+            pl.BlockSpec((step_rows * NEW, columns), lambda i: (i, 0)),
+            pl.BlockSpec((step_rows, context, columns), lambda i: (i, 0, 0)),
+            pl.BlockSpec((kv_heads, 2, step_rows, context), lambda i: (0, 0, i, 0)),
+            pl.BlockSpec((owners * GT, columns), lambda i: (0, 0)),
+            pl.BlockSpec((1, owners * GT), lambda i: (0, 0)),
+            pl.BlockSpec((1, owners * GT), lambda i: (0, 0)),
+        ],
+        out_specs=pl.BlockSpec((kv_heads, step_rows * head_rows, HD), lambda i: (0, i, 0)),
+        compiler_params=pltpu.CompilerParams(vmem_limit_bytes=32 * MIB),
+        cost_estimate=pl.CostEstimate(
+            flops=4 * row_count * head_rows * kv_heads * HD * (context + owners * GT),
+            bytes_accessed=8 * MIB, transcendentals=0,
+        ),
+    )(
+        lengths, query_heads, new_kv.reshape(row_count * NEW, columns), cache_codes, scales,
+        arrived.reshape(owners * GT, columns), sent_rms, sent_rows,
+    )
+    attention = jnp.transpose(
+        attention.reshape(kv_heads, row_count, head_group, NEW, HD), (1, 3, 0, 2, 4)
+    ).reshape(row_count * NEW, kv_heads * head_group * HD)
     rows, depth = attention.shape
     per = n_seq // n_tp
     out_columns = w_out.shape[1]

time: 202 us -> 179 us (0.89)
  matrix products: 16.1 us -> 0 us
  local copies, waits for them, and re-layouts: 15.2 us -> 8.26 us
  Pallas kernels: 160 us -> 166 us
  other arithmetic: 9.88 us -> 4.2 us
    dot_general x6 -> x0, matrix products: 16.1 us -> none  [the longest x1 3.45 us: on_device(): jnp.einsum('rinhk,knd->rinhd', (w_sent * sent_rms).astype(jnp.bfloat16),...]
    pallas_call x0 -> x1, Pallas kernels: none -> 6.57 us  [on_device(): pl.pallas_call(functools.partial(attention_kernel, kv_heads, head_group,...]
    unnamed x17 -> x10, local copies, waits for them, and re-layouts: 9.54 us -> 3.51 us
    reduce_sum x3 -> x0, other arithmetic: 5.4 us -> none  [the longest x1 3.09 us: on_device(): jnp.sum(w_sent, axis=-1)]
    slice x3 -> x1, local copies, waits for them, and re-layouts: 2.37 us -> 0.15 us  [on_device(): sent_rows = jnp.repeat(meta[:, 1, 0], GT)[None, :]]
where the time goes in v2:
time: 179 us; the launch traced here: 178 us
  Pallas kernels  166 us (93%)
  local copies, waits for them, and re-layouts  8.26 us (5%)
  other arithmetic  4.2 us (2%)
    pallas_call x1, Pallas kernels, on_device(): pl.pallas_call(functools.partial(project_kernel, n_grp, n_seq, n_tp), out...  93.7 us
    pallas_call x1, Pallas kernels, on_device(): pl.pallas_call(functools.partial(output_kernel, n_seq, n_tp), out_shape=j...  65.6 us
    pallas_call x1, Pallas kernels, on_device(): pl.pallas_call(functools.partial(attention_kernel, kv_heads, head_group,...  6.57 us

profile of v2, /device:TPU:6, one launch (start us, length us, event | category | flops | bytes accessed | tf_op | source)
XLA Modules:
  0.0 178.5 jit_solution(16119998259543908081)
XLA Ops:
  0.0 0.0 copy-start.1
  0.0 0.5 broadcast.135
  0.5 1.4 reduce.13
  2.0 2.1 %multiply_reduce_fusion = f32[512]{0:T(512)S(1)} fusion(bf16[512,2048]{1,0:T(8,128)(2,1)} %x_ref.1), kind=kLoop, calls=%fused_computation | loop fusion | flops 3145216 | bytes 2099200 | tf_op jit(solution)/shard_map/reduce_sum | solution.py:314
  4.0 0.1 reshape.125
  4.1 0.1 reshape_squeeze.4
  4.2 0.7 reshape.126
  4.9 0.1 add_reduce_fusion
  5.1 0.2 select_reduce_fusion
  5.3 0.1 broadcast_compare_fusion
  5.4 0.1 copy.16
  5.4 0.1 broadcast_in_dim.37
  5.5 0.1 reshape.127
  5.6 0.7 copy.15
  6.3 0.1 broadcast_in_dim.36.rows_ref
  6.4 0.9 reshape.122.new_ref
  7.4 0.1 copy.18.scale_ref
  7.5 0.1 broadcast_in_dim.38
  7.6 0.4 copy.17
  8.0 0.3 and_convert_fusion.pick_ref
  8.2 0.0 copy-done.1
  8.2 0.0 copy-start.3
  8.3 0.0 copy-start.2
  8.3 93.7 %shard_map.100 = (bf16[8,64,512]{2,1,0:T(8,128)(2,1)S(1)}, f32[8,8,128]{2,1,0:T(8,128)S(1)}) custom-call(f32[8,8]{1,0:T(8,128)S(1)} %get-tuple-element.10.match_ref, bf16[512,2048]{1,0:T(8,128)(2,1)S(1)} %copy-done.1, bf16[8192,512]{1,0:T(8,128)(2,1)} %w_ref.2, f32[8,128]{1,0:T(8,128)S(1)} %pad.4.ss_ref, f32[8,8,128]{2,1,0:T(8,128)S(1)} %broadcast_in_dim.36.rows_ref, ...), custom_call_target="tpu_custom_call" | custom-call | flops 4294967296 | bytes 16777216 | tf_op jit(solution)/shard_map/pallas_call | solution.py:322
  102.0 0.1 slice_reduce_fusion
  102.2 0.1 rsqrt.6.rms_ref
  102.3 0.1 broadcast_in_dim.39
  102.3 0.1 broadcast_in_dim_reshape.3.rows_ref
  102.4 0.0 copy-done.3
  102.4 0.3 reshape.120
  102.8 0.2 copy.14
  103.0 0.0 copy-done.2
  103.0 0.0 copy-start
  103.0 2.2 %copy-done = bf16[32,128,512]{2,1,0:T(8,128)(2,1)S(1)} copy-done((bf16[32,128,512]{2,1,0:T(8,128)(2,1)S(1)}, bf16[32,128,512]{2,1,0:T(8,128)(2,1)}, u32[]{:S(2)}) %copy-start) | copy-done | bytes 4194328
  105.2 6.6 %shard_map.101 = bf16[2,1024,128]{2,1,0:T(8,128)(2,1)S(1)} custom-call(s32[32]{0:T(128)S(1)} %copy-done.2, bf16[2,1024,128]{2,1,0:T(8,128)(2,1)S(1)} %bitcast.18, bf16[128,512]{1,0:T(8,128)(2,1)S(1)} %reshape.122.new_ref, bf16[32,128,512]{2,1,0:T(8,128)(2,1)S(1)} %copy-done, f32[2,2,32,128]{3,2,1,0:T(8,128)S(1)} %copy.18.scale_ref, ...), custom_call_target="tpu_custom_call" | custom-call | flops 671088640 | bytes 8388608 | tf_op jit(solution)/shard_map/pallas_call | solution.py:373
  111.7 0.1 copy.21
  111.9 0.2 reshape.131.attn_ref
  112.1 65.6 %shard_map.102 = bf16[128,2048]{1,0:T(8,128)(2,1)S(1)} custom-call(bf16[128,2048]{1,0:T(8,128)(2,1)S(1)} %reshape.131.attn_ref, bf16[2048,2048]{1,0:T(8,128)(2,1)} %w_ref.3), custom_call_target="tpu_custom_call" | custom-call | flops 4294967296 | bytes 16777216 | tf_op jit(solution)/shard_map/pallas_call | solution.py:403
  177.7 0.8 copy.23
  (6 shorter events, 0.1 us)
Async XLA Ops:
  0.0 8.2 %copy-start.1 = (bf16[512,2048]{1,0:T(8,128)(2,1)S(1)}, bf16[512,2048]{1,0:T(8,128)(2,1)}, u32[]{:S(2)}) copy-start(bf16[512,2048]{1,0:T(8,128)(2,1)} %x_ref.1) | copy-start | bytes 6291460
  8.2 94.2 %copy-start.3 = (bf16[32,4,2048]{2,1,0:T(4,128)(2,1)S(1)}, bf16[32,4,2048]{2,1,0:T(4,128)(2,1)}, u32[]{:S(2)}) copy-start(bf16[32,4,2048]{2,1,0:T(4,128)(2,1)} %param.14) | copy-start | bytes 1572868
  8.3 94.7 %copy-start.2 = (s32[32]{0:T(128)S(1)}, s32[32]{0:T(128)}, u32[]{:S(2)}) copy-start(s32[32]{0:T(128)} %lengths_ref.1) | copy-start | bytes 388
  103.0 2.2 %copy-start = (bf16[32,128,512]{2,1,0:T(8,128)(2,1)S(1)}, bf16[32,128,512]{2,1,0:T(8,128)(2,1)}, u32[]{:S(2)}) copy-start(bf16[32,128,512]{2,1,0:T(8,128)(2,1)} %cache_ref.1) | copy-start | bytes 12582916

commit v3 on v2

--- a/solution.py
+++ b/solution.py
@@ -28,11 +28,38 @@
     )
 
 
+def pass_on(z, n, d, acc, mine, landing, send_sem, recv_sem):
+    for way, step in ((0, 1), (1, -1)):
+        @pl.when((d - z) * step > 0)
+        def _():
+            begins = z == (0 if step > 0 else n - 1)
+
+            @pl.when(jnp.logical_not(begins))
+            def _():
+                remote(mine, landing.at[way], send_sem, recv_sem.at[way], tp=z - step).wait_recv()
+                mine[...] = (acc[...] + landing[way].astype(jnp.float32)).astype(jnp.bfloat16)
+
+            @pl.when(begins)
+            def _():
+                mine[...] = acc[...].astype(jnp.bfloat16)
+
+            remote(mine, landing.at[way], send_sem, recv_sem.at[way], tp=z + step).start()
+
+
+def take_in(z, n, acc, landing, recv_sem):
+    for way, begins in ((0, 0), (1, n - 1)):
+        @pl.when(z != begins)
+        def _():
+            other = z - 1 if way == 0 else z + 1
+            remote(landing.at[way], landing.at[way], recv_sem.at[way], recv_sem.at[way], tp=other).wait_recv()
+            acc[...] += landing[way].astype(jnp.float32)
+
+
 def project_kernel(
     n_grp, n_seq, n_tp,
     match_ref, x_ref, w_ref, ss_ref, rows_ref, pick_ref,
     akv_ref, ameta_ref,
-    wbuf, own, pbuf, rbuf, ssbuf, sstot, kvbuf, stage, mstage, kland, mland,
+    wbuf, own, acc, pbuf, rbuf, ssbuf, sstot, kvbuf, stage, mstage, kland, mland,
     local_sem, zs, zr, ps, pr, gs, gr, ds, dr, ss_s, ss_r, ks, kr, ms, mr,
 ):
     me_g, me_s, me_t = lax.axis_index("grp"), lax.axis_index("seq"), lax.axis_index("tp")
@@ -106,7 +133,7 @@
                 copy = remote(mine, mine, gs.at[c, k, 0, e], gr.at[c, k, 0, e], grp=lax.rem(me_g + e, n_grp))
                 copy.start()
                 waits.append(copy)
-    sent = []
+    dest_order = sorted(range(n_tp), key=lambda d: (min(d, n_tp - 1 - d), -d))
     for c in range(chunks):
         for k in range(1, n_tp):
             t = lax.rem(me_t + n_tp - k, n_tp)
@@ -120,20 +147,19 @@
                     )
                     copy.start()
                     waits.append(copy)
-        for k in range(1, n_tp):
-            t = lax.rem(me_t + n_tp - k, n_tp)
-            for j in range(n_seq):
-                s = lax.rem(me_s + n_seq - j, n_seq)
-                for e in range(1, n_grp):
-                    g = lax.rem(me_g + n_grp - e, n_grp)
-                    theirs = wbuf.at[t, rows_of(g, s), cols[c]]
-                    remote(theirs, theirs, gs.at[c, k, j, e], gr.at[c, k, j, e], grp=g).wait_recv()
-            pbuf[k, c] = jnp.dot(
-                x_ref[...], wbuf[t, :, cols[c]], preferred_element_type=jnp.float32
-            ).astype(jnp.bfloat16)
-            copy = remote(pbuf.at[k, c], rbuf.at[k, c], ds.at[c, k], dr.at[c, k], tp=t)
-            copy.start()
-            sent.append(copy)
+        for d in dest_order:
+            k = lax.rem(me_t + n_tp - d, n_tp)
+
+            @pl.when(me_t != d)
+            def _():
+                for j in range(n_seq):
+                    s = lax.rem(me_s + n_seq - j, n_seq)
+                    for e in range(1, n_grp):
+                        g = lax.rem(me_g + n_grp - e, n_grp)
+                        theirs = wbuf.at[d, rows_of(g, s), cols[c]]
+                        remote(theirs, theirs, gs.at[c, k, j, e], gr.at[c, k, j, e], grp=g).wait_recv()
+                acc[...] = jnp.dot(x_ref[...], wbuf[d, :, cols[c]], preferred_element_type=jnp.float32)
+                pass_on(me_t, n_tp, d, acc, pbuf.at[d, c], rbuf.at[:, d, c], ds.at[c, d], dr.at[:, c, d])
 
     total = ss_ref[...]
     for k in range(1, n_tp):
@@ -141,11 +167,9 @@
         total = total + ssbuf[k]
     sstot[...] = total
     for c in range(chunks):
-        acc = own[:, cols[c]]
-        for k in range(1, n_tp):
-            sent[c * (n_tp - 1) + k - 1].wait_recv()
-            acc = acc + rbuf[k, c].astype(jnp.float32)
-        kvbuf[:, cols[c]] = acc.astype(jnp.bfloat16)
+        acc[...] = own[:, cols[c]]
+        take_in(me_t, n_tp, acc, rbuf.at[:, me_t, c], dr.at[:, c, me_t])
+        kvbuf[:, cols[c]] = acc[...].astype(jnp.bfloat16)
 
     out = []
     sub = lax.broadcasted_iota(jnp.int32, (8, 128), 0)
@@ -173,8 +197,13 @@
     for j in range(1, owners):
         akv_ref[j] = kland[j]
         ameta_ref[j] = mland[j]
-    for copy in waits + sent + out:
+    for copy in waits + out:
         copy.wait_send()
+    for c in range(chunks):
+        for d in range(n_tp):
+            @pl.when(me_t != d)
+            def _():
+                remote(pbuf.at[d, c], rbuf.at[0, d, c], ds.at[c, d], dr.at[0, c, d], tp=d).wait_send()
 
 
 def attention_kernel(
@@ -233,12 +262,12 @@
 
 
 def output_kernel(
-    n_seq, n_tp, attn_ref, w_ref, out_ref, wv, held, pbuf, rbuf, local_sem, as_, ar, ds, dr
+    n_seq, n_tp, attn_ref, w_ref, out_ref, wv, held, acc, own, pbuf, rbuf, local_sem, as_, ar, ds, dr
 ):
     me_s, me_t = lax.axis_index("seq"), lax.axis_index("tp")
     per = n_seq // n_tp
     rows, columns = attn_ref.shape[0], w_ref.shape[1]
-    tile = min(512, columns)
+    tile = acc.shape[1]
     local = pltpu.make_async_copy(w_ref, wv, local_sem)
     local.start()
     barrier = pltpu.get_barrier_semaphore()
@@ -263,32 +292,32 @@
 
         @pl.loop(0, columns // tile)
         def _(c):
-            cols = pl.ds(pl.multiple_of(c * tile, tile), tile)
-            pbuf[s, :, cols] = jnp.dot(
-                block[...], wv[:, cols], preferred_element_type=jnp.float32
-            ).astype(jnp.bfloat16)
-
-        @pl.when(dest != me_t)
-        def _():
-            remote(pbuf.at[s], rbuf.at[me_t, sub], ds.at[s], dr.at[me_t, sub], tp=dest).start()
-
-    acc = [
-        pbuf[pl.ds(me_t * per + u, 1)][0].astype(jnp.float32) for u in range(per)
-    ]
-    for k in range(1, n_tp):
-        t = lax.rem(me_t + k, n_tp)
-        for u in range(per):
-            remote(pbuf.at[0], rbuf.at[t, u], ds.at[0], dr.at[t, u], tp=t).wait_recv()
-            acc[u] = acc[u] + rbuf[pl.ds(t, 1), u][0].astype(jnp.float32)
+            acc[...] = jnp.dot(
+                block[...], wv[:, pl.ds(pl.multiple_of(c * tile, tile), tile)], preferred_element_type=jnp.float32
+            )
+
+            @pl.when(dest == me_t)
+            def _():
+                own[sub, c] = acc[...]
+
+            @pl.when(dest != me_t)
+            def _():
+                pass_on(me_t, n_tp, dest, acc, pbuf.at[s, c], rbuf.at[:, s, c], ds.at[s, c], dr.at[:, s, c])
+
     for u in range(per):
-        out_ref[pl.ds(u * rows, rows), :] = acc[u].astype(jnp.bfloat16)
+        for c in range(columns // tile):
+            s = me_t * per + u
+            acc[...] = own[u, c]
+            take_in(me_t, n_tp, acc, rbuf.at[:, s, c], dr.at[:, s, c])
+            out_ref[u * rows : (u + 1) * rows, c * tile : (c + 1) * tile] = acc[...].astype(jnp.bfloat16)
     for copy in gathers:
         copy.wait_send()
     for k in range(1, n_tp):
         t = lax.rem(me_t + k, n_tp)
         for u in range(per):
             s = t * per + u
-            remote(pbuf.at[s], rbuf.at[me_t, u], ds.at[s], dr.at[me_t, u], tp=t).wait_send()
+            for c in range(columns // tile):
+                remote(pbuf.at[s, c], rbuf.at[0, s, c], ds.at[s, c], dr.at[0, s, c], tp=t).wait_send()
 
 
 def on_device(
@@ -332,8 +361,9 @@
         scratch_shapes=[
             pltpu.VMEM((n_tp, features, columns), bf16),
             pltpu.VMEM((tokens, columns), f32),
+            pltpu.VMEM((tokens, width), f32),
             pltpu.VMEM((n_tp, chunks, tokens, width), bf16),
-            pltpu.VMEM((n_tp, chunks, tokens, width), bf16),
+            pltpu.VMEM((2, n_tp, chunks, tokens, width), bf16),
             pltpu.VMEM((n_tp,) + squares.shape, f32),
             pltpu.VMEM(squares.shape, f32),
             pltpu.VMEM((tokens, columns), bf16),
@@ -344,7 +374,7 @@
             dma, dma((chunks, n_tp)), dma((chunks, n_tp)),
             dma((chunks, n_tp, n_seq)), dma((chunks, n_tp, n_seq)),
             dma((chunks, n_tp, n_seq, n_grp)), dma((chunks, n_tp, n_seq, n_grp)),
-            dma((chunks, n_tp)), dma((chunks, n_tp)), dma((n_tp,)), dma((n_tp,)),
+            dma((chunks, n_tp)), dma((2, chunks, n_tp)), dma((n_tp,)), dma((n_tp,)),
             dma((owners,)), dma((owners,)), dma((owners,)), dma((owners,)),
         ],
         compiler_params=pltpu.CompilerParams(
@@ -400,6 +430,8 @@
     rows, depth = attention.shape
     per = n_seq // n_tp
     out_columns = w_out.shape[1]
+    tile = min(512, out_columns)
+    tiles = out_columns // tile
     return pl.pallas_call(
         functools.partial(output_kernel, n_seq, n_tp),
         out_shape=jax.ShapeDtypeStruct((per * rows, out_columns), bf16),
@@ -408,9 +440,11 @@
         scratch_shapes=[
             pltpu.VMEM((depth, out_columns), bf16),
             pltpu.VMEM((n_seq, rows, depth), bf16),
-            pltpu.VMEM((n_seq, rows, out_columns), bf16),
-            pltpu.VMEM((n_tp, per, rows, out_columns), bf16),
-            dma, dma((n_seq,)), dma((n_seq,)), dma((n_seq,)), dma((n_tp, per)),
+            pltpu.VMEM((rows, tile), f32),
+            pltpu.VMEM((per, tiles, rows, tile), f32),
+            pltpu.VMEM((n_seq, tiles, rows, tile), bf16),
+            pltpu.VMEM((2, n_seq, tiles, rows, tile), bf16),
+            dma, dma((n_seq,)), dma((n_seq,)), dma((n_seq, tiles)), dma((2, n_seq, tiles)),
         ],
         compiler_params=pltpu.CompilerParams(
             collective_id=1, has_side_effects=True, vmem_limit_bytes=48 * MIB

time: 179 us -> 169 us (0.944)
  Pallas kernels: 166 us -> 156 us
    pallas_call x1, Pallas kernels: 93.7 us -> 87.8 us  [on_device(): pl.pallas_call(functools.partial(project_kernel, n_grp, n_seq, n_tp), out...]
    pallas_call x1, Pallas kernels: 65.6 us -> 61.5 us  [on_device(): pl.pallas_call(functools.partial(output_kernel, n_seq, n_tp), out_shape=j...]
where the time goes in v3:
time: 169 us; the launch traced here: 168 us
  Pallas kernels  156 us (92%)
  local copies, waits for them, and re-layouts  8.26 us (5%)
  other arithmetic  4.2 us (2%)
    pallas_call x1, Pallas kernels, on_device(): pl.pallas_call(functools.partial(project_kernel, n_grp, n_seq, n_tp), out...  87.8 us
    pallas_call x1, Pallas kernels, on_device(): pl.pallas_call(functools.partial(output_kernel, n_seq, n_tp), out_shape=j...  61.5 us
    pallas_call x1, Pallas kernels, on_device(): pl.pallas_call(functools.partial(attention_kernel, kv_heads, head_group,...  6.57 us
    unnamed x10, local copies, waits for them, and re-layouts  3.51 us

profile of v3, /device:TPU:6, one launch (start us, length us, event | category | flops | bytes accessed | tf_op | source)
XLA Modules:
  0.0 168.4 jit_solution(8791551432827852436)
XLA Ops:
  0.0 0.0 copy-start.1
  0.0 0.5 broadcast.135
  0.5 1.4 reduce.13
  2.0 2.1 %multiply_reduce_fusion = f32[512]{0:T(512)S(1)} fusion(bf16[512,2048]{1,0:T(8,128)(2,1)} %x_ref.1), kind=kLoop, calls=%fused_computation | loop fusion | flops 3145216 | bytes 2099200 | tf_op jit(solution)/shard_map/reduce_sum | solution.py:343
  4.0 0.1 reshape.125
  4.1 0.1 reshape_squeeze.4
  4.2 0.7 reshape.126
  4.9 0.1 add_reduce_fusion
  5.1 0.2 select_reduce_fusion
  5.3 0.1 broadcast_compare_fusion
  5.4 0.1 copy.16
  5.4 0.1 broadcast_in_dim.37
  5.5 0.1 reshape.127
  5.6 0.7 copy.15
  6.3 0.1 broadcast_in_dim.36.rows_ref
  6.4 0.9 reshape.122.new_ref
  7.4 0.1 copy.18.scale_ref
  7.5 0.1 broadcast_in_dim.38
  7.6 0.4 copy.17
  8.0 0.3 and_convert_fusion.pick_ref
  8.2 0.0 copy-done.1
  8.2 0.0 copy-start.3
  8.3 0.0 copy-start.2
  8.3 87.8 %shard_map.100 = (bf16[8,64,512]{2,1,0:T(8,128)(2,1)S(1)}, f32[8,8,128]{2,1,0:T(8,128)S(1)}) custom-call(f32[8,8]{1,0:T(8,128)S(1)} %get-tuple-element.10.match_ref, bf16[512,2048]{1,0:T(8,128)(2,1)S(1)} %copy-done.1, bf16[8192,512]{1,0:T(8,128)(2,1)} %w_ref.2, f32[8,128]{1,0:T(8,128)S(1)} %pad.4.ss_ref, f32[8,8,128]{2,1,0:T(8,128)S(1)} %broadcast_in_dim.36.rows_ref, ...), custom_call_target="tpu_custom_call" | custom-call | flops 4294967296 | bytes 16777216 | tf_op jit(solution)/shard_map/pallas_call | solution.py:351
  96.0 0.1 slice_reduce_fusion
  96.2 0.1 rsqrt.6.rms_ref
  96.3 0.1 broadcast_in_dim.39
  96.4 0.1 broadcast_in_dim_reshape.3.rows_ref
  96.4 0.0 copy-done.3
  96.4 0.3 reshape.120
  96.8 0.2 copy.14
  97.0 0.0 copy-done.2
  97.0 0.0 copy-start
  97.0 2.2 %copy-done = bf16[32,128,512]{2,1,0:T(8,128)(2,1)S(1)} copy-done((bf16[32,128,512]{2,1,0:T(8,128)(2,1)S(1)}, bf16[32,128,512]{2,1,0:T(8,128)(2,1)}, u32[]{:S(2)}) %copy-start) | copy-done | bytes 4194328
  99.2 6.6 %shard_map.101 = bf16[2,1024,128]{2,1,0:T(8,128)(2,1)S(1)} custom-call(s32[32]{0:T(128)S(1)} %copy-done.2, bf16[2,1024,128]{2,1,0:T(8,128)(2,1)S(1)} %bitcast.18, bf16[128,512]{1,0:T(8,128)(2,1)S(1)} %reshape.122.new_ref, bf16[32,128,512]{2,1,0:T(8,128)(2,1)S(1)} %copy-done, f32[2,2,32,128]{3,2,1,0:T(8,128)S(1)} %copy.18.scale_ref, ...), custom_call_target="tpu_custom_call" | custom-call | flops 671088640 | bytes 8388608 | tf_op jit(solution)/shard_map/pallas_call | solution.py:403
  105.8 0.1 copy.21
  105.9 0.2 reshape.131.attn_ref
  106.1 61.5 %shard_map.102 = bf16[128,2048]{1,0:T(8,128)(2,1)S(1)} custom-call(bf16[128,2048]{1,0:T(8,128)(2,1)S(1)} %reshape.131.attn_ref, bf16[2048,2048]{1,0:T(8,128)(2,1)} %w_ref.3), custom_call_target="tpu_custom_call" | custom-call | flops 4294967296 | bytes 16777216 | tf_op jit(solution)/shard_map/pallas_call | solution.py:435
  167.6 0.8 copy.23
  (6 shorter events, 0.1 us)
Async XLA Ops:
  0.0 8.2 %copy-start.1 = (bf16[512,2048]{1,0:T(8,128)(2,1)S(1)}, bf16[512,2048]{1,0:T(8,128)(2,1)}, u32[]{:S(2)}) copy-start(bf16[512,2048]{1,0:T(8,128)(2,1)} %x_ref.1) | copy-start | bytes 6291460
  8.2 88.2 %copy-start.3 = (bf16[32,4,2048]{2,1,0:T(4,128)(2,1)S(1)}, bf16[32,4,2048]{2,1,0:T(4,128)(2,1)}, u32[]{:S(2)}) copy-start(bf16[32,4,2048]{2,1,0:T(4,128)(2,1)} %param.14) | copy-start | bytes 1572868
  8.3 88.7 %copy-start.2 = (s32[32]{0:T(128)S(1)}, s32[32]{0:T(128)}, u32[]{:S(2)}) copy-start(s32[32]{0:T(128)} %lengths_ref.1) | copy-start | bytes 388
  97.0 2.2 %copy-start = (bf16[32,128,512]{2,1,0:T(8,128)(2,1)S(1)}, bf16[32,128,512]{2,1,0:T(8,128)(2,1)}, u32[]{:S(2)}) copy-start(bf16[32,128,512]{2,1,0:T(8,128)(2,1)} %cache_ref.1) | copy-start | bytes 12582916

commit v4 on v3

--- a/solution.py
+++ b/solution.py
@@ -71,6 +71,8 @@
     width = rbuf.shape[-1]
     chunks = w_ref.shape[1] // width
     cols = [slice(c * width, (c + 1) * width) for c in range(chunks)]
+    half = x_ref.shape[0] // 2
+    halves = [slice(0, half), slice(half, 2 * half)]
     waits = []
 
     def rows_of(g, s):
@@ -158,8 +160,12 @@
                         g = lax.rem(me_g + n_grp - e, n_grp)
                         theirs = wbuf.at[d, rows_of(g, s), cols[c]]
                         remote(theirs, theirs, gs.at[c, k, j, e], gr.at[c, k, j, e], grp=g).wait_recv()
-                acc[...] = jnp.dot(x_ref[...], wbuf[d, :, cols[c]], preferred_element_type=jnp.float32)
-                pass_on(me_t, n_tp, d, acc, pbuf.at[d, c], rbuf.at[:, d, c], ds.at[c, d], dr.at[:, c, d])
+                for h, rows in enumerate(halves):
+                    acc[rows] = jnp.dot(x_ref[rows], wbuf[d, :, cols[c]], preferred_element_type=jnp.float32)
+                    pass_on(
+                        me_t, n_tp, d, acc.at[rows], pbuf.at[d, c, rows], rbuf.at[:, d, c, rows],
+                        ds.at[c, d, h], dr.at[:, c, d, h],
+                    )
 
     total = ss_ref[...]
     for k in range(1, n_tp):
@@ -168,7 +174,8 @@
     sstot[...] = total
     for c in range(chunks):
         acc[...] = own[:, cols[c]]
-        take_in(me_t, n_tp, acc, rbuf.at[:, me_t, c], dr.at[:, c, me_t])
+        for h, rows in enumerate(halves):
+            take_in(me_t, n_tp, acc.at[rows], rbuf.at[:, me_t, c, rows], dr.at[:, c, me_t, h])
         kvbuf[:, cols[c]] = acc[...].astype(jnp.bfloat16)
 
     out = []
@@ -203,7 +210,10 @@
         for d in range(n_tp):
             @pl.when(me_t != d)
             def _():
-                remote(pbuf.at[d, c], rbuf.at[0, d, c], ds.at[c, d], dr.at[0, c, d], tp=d).wait_send()
+                for h, rows in enumerate(halves):
+                    remote(
+                        pbuf.at[d, c, rows], rbuf.at[0, d, c, rows], ds.at[c, d, h], dr.at[0, c, d, h], tp=d
+                    ).wait_send()
 
 
 def attention_kernel(
@@ -278,15 +288,36 @@
     pl.semaphore_wait(barrier, n_tp - 1 + n_seq - 1)
 
     gathers = []
-    for j in range(1, n_seq):
-        copy = remote(attn_ref, held.at[j], as_.at[j], ar.at[j], seq=lax.rem(me_s + j, n_seq))
+
+    def gather(src, dst, i, s):
+        copy = remote(src, dst, as_.at[i], ar.at[i], seq=s)
         copy.start()
         gathers.append(copy)
+
+    square = n_seq == 4
+    if square:
+        beside, above = me_s + 1 - 2 * lax.rem(me_s, 2), lax.rem(me_s + 2, 4)
+        sources = [me_s, beside, above, lax.rem(beside + 2, 4)]
+        half = rows // 2
+        gather(attn_ref, held.at[1], 1, beside)
+        gather(attn_ref, held.at[2], 2, above)
+    else:
+        sources = [lax.rem(me_s + n_seq - j, n_seq) for j in range(n_seq)]
+        for j in range(1, n_seq):
+            gather(attn_ref, held.at[j], j, lax.rem(me_s + j, n_seq))
     local.wait()
     for j in range(n_seq):
-        s = lax.rem(me_s + n_seq - j, n_seq)
+        s = sources[j]
         dest, sub = s // per, lax.rem(s, per)
-        if j > 0:
+        if square and j == 1:
+            gathers[0].wait_recv()
+            gather(held.at[1, :half], held.at[3, :half], 3, above)
+            gathers[1].wait_recv()
+            gather(held.at[2, half:], held.at[3, half:], 4, beside)
+        elif square and j == 3:
+            gathers[2].wait_recv()
+            gathers[3].wait_recv()
+        elif j > 0 and not square:
             gathers[j - 1].wait_recv()
         block = attn_ref if j == 0 else held.at[j]
 
@@ -374,7 +405,7 @@
             dma, dma((chunks, n_tp)), dma((chunks, n_tp)),
             dma((chunks, n_tp, n_seq)), dma((chunks, n_tp, n_seq)),
             dma((chunks, n_tp, n_seq, n_grp)), dma((chunks, n_tp, n_seq, n_grp)),
-            dma((chunks, n_tp)), dma((2, chunks, n_tp)), dma((n_tp,)), dma((n_tp,)),
+            dma((chunks, n_tp, 2)), dma((2, chunks, n_tp, 2)), dma((n_tp,)), dma((n_tp,)),
             dma((owners,)), dma((owners,)), dma((owners,)), dma((owners,)),
         ],
         compiler_params=pltpu.CompilerParams(
@@ -444,7 +475,7 @@
             pltpu.VMEM((per, tiles, rows, tile), f32),
             pltpu.VMEM((n_seq, tiles, rows, tile), bf16),
             pltpu.VMEM((2, n_seq, tiles, rows, tile), bf16),
-            dma, dma((n_seq,)), dma((n_seq,)), dma((n_seq, tiles)), dma((2, n_seq, tiles)),
+            dma, dma((n_seq + 1,)), dma((n_seq + 1,)), dma((n_seq, tiles)), dma((2, n_seq, tiles)),
         ],
         compiler_params=pltpu.CompilerParams(
             collective_id=1, has_side_effects=True, vmem_limit_bytes=48 * MIB

time: 169 us -> 170 us (level)
    pallas_call x1, Pallas kernels: 61.5 us -> 64.6 us  [on_device(): pl.pallas_call(functools.partial(output_kernel, n_seq, n_tp), out_shape=j...]
where the time goes in v4:
time: 170 us
  Pallas kernels  157 us (92%)
  local copies, waits for them, and re-layouts  8.26 us (5%)
  other arithmetic  4.2 us (2%)
    pallas_call x1, Pallas kernels, on_device(): pl.pallas_call(functools.partial(project_kernel, n_grp, n_seq, n_tp), out...  86.1 us
    pallas_call x1, Pallas kernels, on_device(): pl.pallas_call(functools.partial(output_kernel, n_seq, n_tp), out_shape=j...  64.6 us
    pallas_call x1, Pallas kernels, on_device(): pl.pallas_call(functools.partial(attention_kernel, kv_heads, head_group,...  6.57 us
    unnamed x10, local copies, waits for them, and re-layouts  3.51 us

profile of v4, /device:TPU:6, one launch (start us, length us, event | category | flops | bytes accessed | tf_op | source)
XLA Modules:
  0.0 169.9 jit_solution(15430507629203435515)
XLA Ops:
  0.0 0.0 copy-start.1
  0.0 0.5 broadcast.135
  0.5 1.4 reduce.13
  2.0 2.1 %multiply_reduce_fusion = f32[512]{0:T(512)S(1)} fusion(bf16[512,2048]{1,0:T(8,128)(2,1)} %x_ref.1), kind=kLoop, calls=%fused_computation | loop fusion | flops 3145216 | bytes 2099200 | tf_op jit(solution)/shard_map/reduce_sum | solution.py:374
  4.0 0.1 reshape.125
  4.1 0.1 reshape_squeeze.4
  4.2 0.7 reshape.126
  4.9 0.1 add_reduce_fusion
  5.1 0.2 select_reduce_fusion
  5.3 0.1 broadcast_compare_fusion
  5.4 0.1 copy.16
  5.4 0.1 broadcast_in_dim.37
  5.5 0.1 reshape.127
  5.6 0.7 copy.15
  6.3 0.1 broadcast_in_dim.36.rows_ref
  6.4 0.9 reshape.122.new_ref
  7.4 0.1 copy.18.scale_ref
  7.5 0.1 broadcast_in_dim.38
  7.6 0.4 copy.17
  8.0 0.3 and_convert_fusion.pick_ref
  8.2 0.0 copy-done.1
  8.2 0.0 copy-start.3
  8.3 0.0 copy-start.2
  8.3 86.1 %shard_map.100 = (bf16[8,64,512]{2,1,0:T(8,128)(2,1)S(1)}, f32[8,8,128]{2,1,0:T(8,128)S(1)}) custom-call(f32[8,8]{1,0:T(8,128)S(1)} %get-tuple-element.10.match_ref, bf16[512,2048]{1,0:T(8,128)(2,1)S(1)} %copy-done.1, bf16[8192,512]{1,0:T(8,128)(2,1)} %w_ref.2, f32[8,128]{1,0:T(8,128)S(1)} %pad.4.ss_ref, f32[8,8,128]{2,1,0:T(8,128)S(1)} %broadcast_in_dim.36.rows_ref, ...), custom_call_target="tpu_custom_call" | custom-call | flops 4294967296 | bytes 16777216 | tf_op jit(solution)/shard_map/pallas_call | solution.py:382
  94.4 0.1 slice_reduce_fusion
  94.6 0.1 rsqrt.6.rms_ref
  94.6 0.1 broadcast_in_dim.39
  94.7 0.1 broadcast_in_dim_reshape.3.rows_ref
  94.8 0.0 copy-done.3
  94.8 0.3 reshape.120
  95.1 0.2 copy.14
  95.3 0.0 copy-done.2
  95.3 0.0 copy-start
  95.4 2.2 %copy-done = bf16[32,128,512]{2,1,0:T(8,128)(2,1)S(1)} copy-done((bf16[32,128,512]{2,1,0:T(8,128)(2,1)S(1)}, bf16[32,128,512]{2,1,0:T(8,128)(2,1)}, u32[]{:S(2)}) %copy-start) | copy-done | bytes 4194328
  97.5 6.6 %shard_map.101 = bf16[2,1024,128]{2,1,0:T(8,128)(2,1)S(1)} custom-call(s32[32]{0:T(128)S(1)} %copy-done.2, bf16[2,1024,128]{2,1,0:T(8,128)(2,1)S(1)} %bitcast.18, bf16[128,512]{1,0:T(8,128)(2,1)S(1)} %reshape.122.new_ref, bf16[32,128,512]{2,1,0:T(8,128)(2,1)S(1)} %copy-done, f32[2,2,32,128]{3,2,1,0:T(8,128)S(1)} %copy.18.scale_ref, ...), custom_call_target="tpu_custom_call" | custom-call | flops 671088640 | bytes 8388608 | tf_op jit(solution)/shard_map/pallas_call | solution.py:434
  104.1 0.1 copy.21
  104.2 0.2 reshape.131.attn_ref
  104.5 64.6 %shard_map.102 = bf16[128,2048]{1,0:T(8,128)(2,1)S(1)} custom-call(bf16[128,2048]{1,0:T(8,128)(2,1)S(1)} %reshape.131.attn_ref, bf16[2048,2048]{1,0:T(8,128)(2,1)} %w_ref.3), custom_call_target="tpu_custom_call" | custom-call | flops 4294967296 | bytes 16777216 | tf_op jit(solution)/shard_map/pallas_call | solution.py:466
  169.1 0.8 copy.23
  (6 shorter events, 0.1 us)
Async XLA Ops:
  0.0 8.2 %copy-start.1 = (bf16[512,2048]{1,0:T(8,128)(2,1)S(1)}, bf16[512,2048]{1,0:T(8,128)(2,1)}, u32[]{:S(2)}) copy-start(bf16[512,2048]{1,0:T(8,128)(2,1)} %x_ref.1) | copy-start | bytes 6291460
  8.2 86.5 %copy-start.3 = (bf16[32,4,2048]{2,1,0:T(4,128)(2,1)S(1)}, bf16[32,4,2048]{2,1,0:T(4,128)(2,1)}, u32[]{:S(2)}) copy-start(bf16[32,4,2048]{2,1,0:T(4,128)(2,1)} %param.14) | copy-start | bytes 1572868
  8.3 87.1 %copy-start.2 = (s32[32]{0:T(128)S(1)}, s32[32]{0:T(128)}, u32[]{:S(2)}) copy-start(s32[32]{0:T(128)} %lengths_ref.1) | copy-start | bytes 388
  95.3 2.2 %copy-start = (bf16[32,128,512]{2,1,0:T(8,128)(2,1)S(1)}, bf16[32,128,512]{2,1,0:T(8,128)(2,1)}, u32[]{:S(2)}) copy-start(bf16[32,128,512]{2,1,0:T(8,128)(2,1)} %cache_ref.1) | copy-start | bytes 12582916

commit v5 on v3

--- a/solution.py
+++ b/solution.py
@@ -430,7 +430,7 @@
     rows, depth = attention.shape
     per = n_seq // n_tp
     out_columns = w_out.shape[1]
-    tile = min(512, out_columns)
+    tile = min(1024, out_columns)
     tiles = out_columns // tile
     return pl.pallas_call(
         functools.partial(output_kernel, n_seq, n_tp),

time: 169 us -> 175 us (1.036)
  Pallas kernels: 156 us -> 162 us
    pallas_call x1, Pallas kernels: 61.5 us -> 67.3 us  [on_device(): pl.pallas_call(functools.partial(output_kernel, n_seq, n_tp), out_shape=j...]
where the time goes in v5:
time: 175 us; the launch traced here: 174 us
  Pallas kernels  162 us (93%)
  local copies, waits for them, and re-layouts  8.26 us (5%)
  other arithmetic  4.2 us (2%)
    pallas_call x1, Pallas kernels, on_device(): pl.pallas_call(functools.partial(project_kernel, n_grp, n_seq, n_tp), out...  87.8 us
    pallas_call x1, Pallas kernels, on_device(): pl.pallas_call(functools.partial(output_kernel, n_seq, n_tp), out_shape=j...  67.3 us
    pallas_call x1, Pallas kernels, on_device(): pl.pallas_call(functools.partial(attention_kernel, kv_heads, head_group,...  6.57 us
    unnamed x10, local copies, waits for them, and re-layouts  3.51 us

profile of v5, /device:TPU:6, one launch (start us, length us, event | category | flops | bytes accessed | tf_op | source)
XLA Modules:
  0.0 174.2 jit_solution(11343303662095692946)
XLA Ops:
  0.0 0.0 copy-start.1
  0.0 0.5 broadcast.135
  0.5 1.4 reduce.13
  2.0 2.1 %multiply_reduce_fusion = f32[512]{0:T(512)S(1)} fusion(bf16[512,2048]{1,0:T(8,128)(2,1)} %x_ref.1), kind=kLoop, calls=%fused_computation | loop fusion | flops 3145216 | bytes 2099200 | tf_op jit(solution)/shard_map/reduce_sum | solution.py:343
  4.0 0.1 reshape.125
  4.1 0.1 reshape_squeeze.4
  4.2 0.7 reshape.126
  4.9 0.1 add_reduce_fusion
  5.1 0.2 select_reduce_fusion
  5.3 0.1 broadcast_compare_fusion
  5.4 0.1 copy.16
  5.4 0.1 broadcast_in_dim.37
  5.5 0.1 reshape.127
  5.6 0.7 copy.15
  6.3 0.1 broadcast_in_dim.36.rows_ref
  6.4 0.9 reshape.122.new_ref
  7.4 0.1 copy.18.scale_ref
  7.5 0.1 broadcast_in_dim.38
  7.6 0.4 copy.17
  8.0 0.3 and_convert_fusion.pick_ref
  8.2 0.0 copy-done.1
  8.2 0.0 copy-start.3
  8.3 0.0 copy-start.2
  8.3 87.8 %shard_map.100 = (bf16[8,64,512]{2,1,0:T(8,128)(2,1)S(1)}, f32[8,8,128]{2,1,0:T(8,128)S(1)}) custom-call(f32[8,8]{1,0:T(8,128)S(1)} %get-tuple-element.10.match_ref, bf16[512,2048]{1,0:T(8,128)(2,1)S(1)} %copy-done.1, bf16[8192,512]{1,0:T(8,128)(2,1)} %w_ref.2, f32[8,128]{1,0:T(8,128)S(1)} %pad.4.ss_ref, f32[8,8,128]{2,1,0:T(8,128)S(1)} %broadcast_in_dim.36.rows_ref, ...), custom_call_target="tpu_custom_call" | custom-call | flops 4294967296 | bytes 16777216 | tf_op jit(solution)/shard_map/pallas_call | solution.py:351
  96.0 0.1 slice_reduce_fusion
  96.2 0.1 rsqrt.6.rms_ref
  96.3 0.1 broadcast_in_dim.39
  96.4 0.1 broadcast_in_dim_reshape.3.rows_ref
  96.4 0.0 copy-done.3
  96.4 0.3 reshape.120
  96.8 0.2 copy.14
  97.0 0.0 copy-done.2
  97.0 0.0 copy-start
  97.0 2.2 %copy-done = bf16[32,128,512]{2,1,0:T(8,128)(2,1)S(1)} copy-done((bf16[32,128,512]{2,1,0:T(8,128)(2,1)S(1)}, bf16[32,128,512]{2,1,0:T(8,128)(2,1)}, u32[]{:S(2)}) %copy-start) | copy-done | bytes 4194328
  99.2 6.6 %shard_map.101 = bf16[2,1024,128]{2,1,0:T(8,128)(2,1)S(1)} custom-call(s32[32]{0:T(128)S(1)} %copy-done.2, bf16[2,1024,128]{2,1,0:T(8,128)(2,1)S(1)} %bitcast.18, bf16[128,512]{1,0:T(8,128)(2,1)S(1)} %reshape.122.new_ref, bf16[32,128,512]{2,1,0:T(8,128)(2,1)S(1)} %copy-done, f32[2,2,32,128]{3,2,1,0:T(8,128)S(1)} %copy.18.scale_ref, ...), custom_call_target="tpu_custom_call" | custom-call | flops 671088640 | bytes 8388608 | tf_op jit(solution)/shard_map/pallas_call | solution.py:403
  105.8 0.1 copy.21
  105.9 0.2 reshape.131.attn_ref
  106.1 67.3 %shard_map.102 = bf16[128,2048]{1,0:T(8,128)(2,1)S(1)} custom-call(bf16[128,2048]{1,0:T(8,128)(2,1)S(1)} %reshape.131.attn_ref, bf16[2048,2048]{1,0:T(8,128)(2,1)} %w_ref.3), custom_call_target="tpu_custom_call" | custom-call | flops 4294967296 | bytes 16777216 | tf_op jit(solution)/shard_map/pallas_call | solution.py:435
  173.4 0.8 copy.23
  (6 shorter events, 0.1 us)
Async XLA Ops:
  0.0 8.2 %copy-start.1 = (bf16[512,2048]{1,0:T(8,128)(2,1)S(1)}, bf16[512,2048]{1,0:T(8,128)(2,1)}, u32[]{:S(2)}) copy-start(bf16[512,2048]{1,0:T(8,128)(2,1)} %x_ref.1) | copy-start | bytes 6291460
  8.2 88.2 %copy-start.3 = (bf16[32,4,2048]{2,1,0:T(4,128)(2,1)S(1)}, bf16[32,4,2048]{2,1,0:T(4,128)(2,1)}, u32[]{:S(2)}) copy-start(bf16[32,4,2048]{2,1,0:T(4,128)(2,1)} %param.14) | copy-start | bytes 1572868
  8.3 88.7 %copy-start.2 = (s32[32]{0:T(128)S(1)}, s32[32]{0:T(128)}, u32[]{:S(2)}) copy-start(s32[32]{0:T(128)} %lengths_ref.1) | copy-start | bytes 388
  97.0 2.2 %copy-start = (bf16[32,128,512]{2,1,0:T(8,128)(2,1)S(1)}, bf16[32,128,512]{2,1,0:T(8,128)(2,1)}, u32[]{:S(2)}) copy-start(bf16[32,128,512]{2,1,0:T(8,128)(2,1)} %cache_ref.1) | copy-start | bytes 12582916
